TPU v7x, 32 devices: a whole 2x2x4 slice. The times are simulated.
32 devices in a mesh: ctx: 2 (over x), inner: 16 (over z, y, core).
Axes of the slice: x: 2, y: 2, z: 4, core: 2. Of those that a mesh axis runs over, the one named last changes fastest.
Arguments:
- gate_input: float32 [4096, 768], P(('ctx', 'inner')), may hold values from -6 to 6
- value_input: float32 [4096, 768], P(('ctx', 'inner')), may hold values from -6 to 6
- filter_taps: float32 [2048, 768], P('inner'), may hold values from -0.125 to 0.125
- decay_rate: float32 [8, 768], replicated, may hold values from 9.765625e-06 to 0.11, as said below
- mode_coeff: float32 [8, 768], replicated, may hold values from -0.09375 to 0.09375
- boundary_keep: float32 [1, 8, 768], replicated, may hold values from 0.6 to 1
- cotangent: float32 [4096, 768], P(('ctx', 'inner')), may hold values from -6 to 6
Outputs:
- mixed_out: float32 [4096, 768], P(('ctx', 'inner'))
- grad_gate: float32 [4096, 768], P(('ctx', 'inner'))
- grad_value: float32 [4096, 768], P(('ctx', 'inner'))
- grad_filter: float32 [2048, 768], P('inner')
Inputs may be any that keep to these rules, and one draw needn't show every extreme that they name: Each decay_rate lies either between 7.6e-07 and 2.3e-05 (a slow mode) or between 0.02 and 0.1 (a fast mode); the mode keeps exp(-decay_rate) of its state a token.
All inputs are finite; a program needn't handle non-finite values.
Results may differ from a plain program's by a relative error of at most 0.00012.
Values sent between devices are 32-bit elements; how exact they have to be, the bound alone decides.
A program may use at most 64 MiB of HBM per device.

v0:
```python
import math

import jax
import jax.numpy as jnp
from jax import lax
from jax.sharding import PartitionSpec as P

FULL_PRECISION = lax.Precision.HIGHEST


def prefix(part, axis, combine, identity, reverse):
    count = lax.axis_size(axis)
    place = lax.axis_index(axis)
    ahead = count - 1 - place if reverse else place
    gathered = jax.tree.map(lambda a: lax.all_gather(a, axis), part)
    state = jax.tree.map(lambda a, e: jnp.zeros_like(a) + jnp.asarray(e, a.dtype), part, identity)

    def one(hop, state):
        source = count - 1 - hop if reverse else hop
        return combine(
            state, jax.tree.map(lambda a: lax.dynamic_index_in_dim(a, source, 0, False), gathered)
        )

    return lax.fori_loop(0, ahead, one, state)


def turn_table(left_index, right_index, period):
    phase = (left_index * right_index % period).astype(jnp.float32) * (2.0 * math.pi / period)
    return (jnp.cos(phase), jnp.sin(phase))


def ahead_table(cosine, sine):
    return jnp.stack([jnp.stack([cosine, sine], 0), jnp.stack([-sine, cosine], 0)], 0)


def behind_table(cosine, sine):
    return jnp.stack([jnp.stack([cosine, -sine], 0), jnp.stack([sine, cosine], 0)], 0)


def contract(form, table, data):
    return jnp.einsum(form, table, data, precision=FULL_PRECISION)


def combine_links(earlier, later_link):
    return (later_link[0] * earlier[0], later_link[0] * earlier[1] + later_link[1])


def carried_mode_state(decay_factors, partial_terms, backward_pass):
    unit_links = jnp.ones_like(decay_factors)
    blank_terms = jnp.zeros_like(partial_terms)
    summed_total = lax.psum(partial_terms, "inner")
    return prefix(
        (decay_factors, summed_total),
        "ctx",
        combine_links,
        (unit_links, blank_terms),
        backward_pass,
    )[1]


def shards(gate_input, value_input, filter_taps, decay_rate, mode_coeff, boundary_keep, cotangent):
    tok_dev = value_input.shape[0]
    inner_count = lax.axis_size("inner")
    ctx_count = lax.axis_size("ctx")
    group_len = tok_dev * inner_count
    fft_len = 2 * group_len
    row_count = 2 * inner_count
    col_count = tok_dev // inner_count
    inner_idx = lax.axis_index("inner")
    ctx_idx = lax.axis_index("ctx")
    row_range = jnp.arange(row_count, dtype=jnp.int32)
    inner_range = jnp.arange(inner_count, dtype=jnp.int32)
    tok_range = jnp.arange(tok_dev, dtype=jnp.int32)
    owner_of_row = row_range // 2
    mirrored_label = jnp.where(owner_of_row == 0, inner_count, row_count - owner_of_row)
    row_label = jnp.where(row_range % 2 == 0, owner_of_row, mirrored_label)
    cos_rows, sin_rows = turn_table(row_label[:, None], inner_range[None, :], row_count)
    rows_table = ahead_table(cos_rows, sin_rows)
    col_index = inner_idx * col_count + jnp.arange(col_count, dtype=jnp.int32)
    cos_twist, sin_twist = turn_table(row_label[:, None, None], col_index[None, :, None], fft_len)
    cos_line, sin_line = turn_table(tok_range[:, None], tok_range[None, :], tok_dev)
    line_ahead = ahead_table(cos_line, sin_line)
    line_behind = behind_table(cos_line, sin_line)
    own_rows = lax.dynamic_slice_in_dim(row_label, 2 * inner_idx, 2, 0)
    cos_untwist, sin_untwist = turn_table(
        own_rows[:, None, None], tok_range[None, :, None], fft_len
    )
    cos_back, sine_reverse = turn_table(inner_range[:, None], row_label[None, :], row_count)
    back_table = behind_table(cos_back, sine_reverse)

    def to_spectrum(signals):
        stacked = jnp.stack(signals, 0)[:, None]
        columns = lax.all_to_all(stacked, "inner", split_axis=2, concat_axis=1, tiled=True)
        count = len(signals)
        parts = contract("pqki,qijc->pkjc", rows_table[:, :count], columns)
        turned = jnp.stack(
            [
                parts[0] * cos_twist + parts[1] * sin_twist,
                parts[1] * cos_twist - parts[0] * sin_twist,
            ],
            0,
        )
        spread = lax.all_to_all(turned, "inner", split_axis=1, concat_axis=2, tiled=True)
        return contract("pqkj,qbjc->pbkc", line_ahead, spread)

    def from_spectrum(spec, keep_imag):
        line = contract("pqjk,qbkc->pbjc", line_behind, spec)
        turned = jnp.stack(
            [
                line[0] * cos_untwist - line[1] * sin_untwist,
                line[1] * cos_untwist + line[0] * sin_untwist,
            ],
            0,
        )
        back = lax.all_to_all(turned, "inner", split_axis=2, concat_axis=1, tiled=True)
        count = 2 if keep_imag else 1
        row_values = contract("pqik,qkjc->pijc", back_table[:count], back) * (1.0 / fft_len)
        joined = lax.all_to_all(row_values, "inner", split_axis=1, concat_axis=2, tiled=True)
        return joined[:, 0]

    def mirror_rows(spec):
        flipped = spec[:, ::-1]
        rolled = jnp.roll(flipped, 1, axis=1)
        leading_device = jnp.stack([rolled[0], flipped[1]], 0)
        return jnp.where(inner_idx == 0, leading_device, flipped[::-1])

    def times_kernel_conj(kern, spec):
        return jnp.stack(
            [kern[0] * spec[0] + kern[1] * spec[1], kern[0] * spec[1] - kern[1] * spec[0]], 0
        )

    positions = (inner_idx * tok_dev + tok_range).astype(jnp.float32)
    rate_wide = decay_rate[:, None, :]
    coeff_wide = mode_coeff[:, None, :]
    to_end_pow = jnp.exp(-rate_wide * (group_len - 1.0 - positions)[None, :, None])
    from_start_pow = coeff_wide * jnp.exp(-rate_wide * (positions + 1.0)[None, :, None])
    tail_part = jnp.sum(coeff_wide * jnp.exp(-rate_wide * positions[None, :, None]), 0)
    group_decay = jnp.exp(-decay_rate * float(group_len))
    keep_full = jnp.concatenate(
        [boundary_keep, jnp.ones((1,) + boundary_keep.shape[1:], jnp.float32)], 0
    )
    keep_row = lax.dynamic_index_in_dim(keep_full, ctx_idx, 0, keepdims=False)
    link_decay = keep_row * group_decay
    kernel = filter_taps + tail_part
    kern_spec = to_spectrum((kernel,))
    mix_grad = cotangent * gate_input
    packed = to_spectrum((value_input, mix_grad))
    mirror_real = mirror_rows(packed[0])
    mirror_imag = mirror_rows(packed[1])
    val_spec = jnp.stack([0.5 * (packed[0] + mirror_real), 0.5 * (packed[1] - mirror_imag)], 0)
    grad_spec = jnp.stack([0.5 * (packed[1] + mirror_imag), 0.5 * (mirror_real - packed[0])], 0)
    ahead = jnp.stack(
        [
            kern_spec[0] * val_spec[0] - kern_spec[1] * val_spec[1],
            kern_spec[0] * val_spec[1] + kern_spec[1] * val_spec[0],
        ],
        0,
    )
    behind = times_kernel_conj(kern_spec, grad_spec)
    both_parts = from_spectrum(jnp.stack([ahead[0] - behind[1], ahead[1] + behind[0]], 0), True)
    inside = both_parts[0]
    through = both_parts[1]
    local_sums = jnp.sum(to_end_pow * value_input[None], 1)
    starts = carried_mode_state(link_decay, keep_row * local_sums, False)
    mixture = inside + jnp.sum(from_start_pow * starts[:, None, :], 0)
    mixed_out = gate_input * mixture
    grad_gate = cotangent * mixture
    pull_terms = jnp.sum(from_start_pow * mix_grad[None], 1)
    later_state = carried_mode_state(link_decay, pull_terms, True)
    grad_value = through + jnp.sum(to_end_pow * (keep_row * later_state)[:, None, :], 0)
    corr = times_kernel_conj(val_spec, grad_spec)
    share_spec = lax.psum_scatter(corr, "ctx", scatter_dimension=3, tiled=True)
    share_grad = from_spectrum(share_spec, False)[0]
    grad_filter = lax.all_gather(share_grad, "ctx", axis=1, tiled=True)
    grad_scale = 1.0 / math.sqrt(group_len * ctx_count)
    return (mixed_out, grad_gate, grad_value, grad_filter * grad_scale)


def solution(mesh):
    placed = (
        P(("ctx", "inner"), None),
        P(("ctx", "inner"), None),
        P("inner", None),
        P(),
        P(),
        P(),
        P(("ctx", "inner"), None),
    )
    return jax.shard_map(
        shards,
        mesh=mesh,
        in_specs=placed,
        out_specs=(
            P(("ctx", "inner"), None),
            P(("ctx", "inner"), None),
            P(("ctx", "inner"), None),
            P("inner", None),
        ),
        check_vma=False,
    )
```

profile of v0, /device:TPU:0, one launch (start us, length us, event | category | flops | bytes accessed | tf_op | source)
XLA Modules:
  0.0 421.3 jit_solution(13700637554054226733)
XLA Ops:
  9.7 5.4 %all-gather = f32[16,768]{1,0:T(8,128)S(1)} all-gather(f32[8,768]{1,0:T(8,128)S(1)} %get-tuple-element.187), channel_id=2, replica_groups=mesh['ctx'=2,'inner'=16] {'ctx'}, dimensions={0}, use_global_device_ids=true | all-gather | bytes 73728 | tf_op jit(solution)/shard_map/all_gather | solution.py:15
  15.1 60.9 %psum.14 = f32[1,8,768]{2,1,0:T(8,128)S(1)} all-reduce(f32[1,8,768]{2,1,0:T(8,128)S(1)} %get-tuple-element.186), channel_id=1, replica_groups=mesh['ctx'=2,'inner'=16] {'inner'}, use_global_device_ids=true, to_apply=%region_2.3 | all-reduce | flops 6144 | bytes 49152 | tf_op jit(solution)/shard_map/psum | solution.py:51
  76.0 4.5 %all_gather.26 = f32[2,8,768]{2,1,0:T(8,128)S(1)} all-gather(f32[1,8,768]{2,1,0:T(8,128)S(1)} %psum.14), channel_id=1, replica_groups=mesh['ctx'=2,'inner'=16] {'ctx'}, dimensions={0}, use_global_device_ids=true | all-gather | bytes 73728 | tf_op jit(solution)/shard_map/all_gather | solution.py:15
  89.7 10.0 %all-to-all-done = f32[1,1,128,768]{3,1,0,2:T(1,128)S(1)} async-done(((f32[1,1,128,768]{3,1,0,2:T(1,128)}), f32[1,1,128,768]{3,1,0,2:T(1,128)S(1)}, u32[]{:S(2)}, u32[]{:S(2)}) %all-to-all-start) | async-done | bytes 393248 | tf_op jit(solution)/shard_map/all_to_all | solution.py:93
  105.0 17.0 %all-to-all-done.2 = f32[2,1,128,768]{3,0,1,2:T(2,128)S(1)} async-done(((f32[2,1,128,768]{3,0,1,2:T(2,128)}), f32[2,1,128,768]{3,0,1,2:T(2,128)S(1)}, u32[]{:S(2)}, u32[]{:S(2)}) %all-to-all-start.2) | async-done | bytes 786464 | tf_op jit(solution)/shard_map/all_to_all | solution.py:93
  127.6 5.6 %all-to-all-start.3 = ((f32[2,32,8,768]{3,2,0,1:T(8,128)}), f32[2,32,8,768]{3,2,0,1:T(8,128)S(1)}, u32[]{:S(2)}, u32[]{:S(2)}) async-start(f32[2,32,8,768]{3,2,0,1:T(8,128)} %copy.98), calls=%async_computation.3 | async-start | bytes 3145728 | tf_op jit(solution)/shard_map/all_to_all | solution.py:103
  135.5 29.7 %all-to-all-done.3 = f32[2,32,8,768]{3,2,0,1:T(8,128)S(1)} async-done(((f32[2,32,8,768]{3,2,0,1:T(8,128)}), f32[2,32,8,768]{3,2,0,1:T(8,128)S(1)}, u32[]{:S(2)}, u32[]{:S(2)}) %all-to-all-start.3) | async-done | bytes 1572896 | tf_op jit(solution)/shard_map/all_to_all | solution.py:103
  165.2 9.2 %all-to-all-start.1 = ((f32[2,32,8,768]{3,2,0,1:T(8,128)}), f32[2,32,8,768]{3,2,0,1:T(8,128)}, u32[]{:S(2)}, u32[]{:S(2)}) async-start(f32[2,32,8,768]{3,2,0,1:T(8,128)} %copy.90), calls=%async_computation.1 | async-start | bytes 3145728 | tf_op jit(solution)/shard_map/all_to_all | solution.py:103
  179.1 4.3 %rev.8 = f32[2,128,768]{1,2,0:T(8,128)} reverse(f32[2,128,768]{1,2,0:T(8,128)S(1)} %get-tuple-element.173), dimensions={0,1} | reverse | bytes 1572864 | tf_op jit(solution)/shard_map/rev | solution.py:125
  184.6 4.3 %rev.9 = f32[2,128,768]{1,2,0:T(8,128)} reverse(f32[2,128,768]{1,2,0:T(8,128)S(1)} %get-tuple-element.174), dimensions={0,1} | reverse | bytes 1572864 | tf_op jit(solution)/shard_map/rev | solution.py:125
  189.9 16.5 %all-to-all-done.1 = f32[2,32,8,768]{3,2,0,1:T(8,128)} async-done(((f32[2,32,8,768]{3,2,0,1:T(8,128)}), f32[2,32,8,768]{3,2,0,1:T(8,128)}, u32[]{:S(2)}, u32[]{:S(2)}) %all-to-all-start.1) | async-done | bytes 1572896 | tf_op jit(solution)/shard_map/all_to_all | solution.py:103
  206.4 5.3 %fusion.7 = f32[2,2,128,768]{2,3,0,1:T(8,128)} fusion(f32[1,2,128,128]{3,2,1,0:T(8,128)} %copy-done.7, f32[1,2,128,128]{3,2,1,0:T(8,128)} %copy-done.8, f32[2,2,16,8,768]{4,3,0,1,2:T(8,128)} %bitcast.18), kind=kOutput, calls=%fused_computation.25 | convolution fusion | flops 1208025088 | bytes 3407872 | tf_op jit(solution)/shard_map/pqkj,qbjc->pbkc/dot_general | solution.py:41
  211.7 7.2 %slice.123 = f32[2,127,768]{1,2,0:T(8,128)} reverse(f32[2,127,768]{1,2,0:T(8,128)} %slice.152), dimensions={1} | reverse | bytes 1560576 | tf_op jit(solution)/shard_map/jit(_roll_static)/slice | solution.py:123
  218.8 7.1 %slice.132 = f32[2,127,768]{1,2,0:T(8,128)} reverse(f32[2,127,768]{1,2,0:T(8,128)} %slice.157), dimensions={1} | reverse | bytes 1560576 | tf_op jit(solution)/shard_map/jit(_roll_static)/slice | solution.py:123
  242.2 9.6 %all-to-all-start.4 = ((f32[2,2,128,768]{3,0,1,2:T(2,128)}), f32[2,2,128,768]{3,0,1,2:T(2,128)S(1)}, u32[]{:S(2)}, u32[]{:S(2)}) async-start(f32[2,2,128,768]{3,0,1,2:T(2,128)} %copy.102), calls=%async_computation.4 | async-start | bytes 3145728 | tf_op jit(solution)/shard_map/all_to_all | solution.py:115
  251.8 17.4 %reduce-scatter.2.cloned.1.call-done = f32[2,2,128,384]{2,3,1,0:T(8,128)} async-done(((f32[2,2,128,768]{2,3,1,0:T(8,128)}), f32[2,2,128,384]{2,3,1,0:T(8,128)}) %reduce-scatter.2.cloned.1.call-update) | async-done | bytes 786448 | tf_op jit(solution)/shard_map/reduce_scatter | solution.py:172
  272.5 11.2 %all-to-all-done.4 = f32[2,2,128,768]{3,0,1,2:T(2,128)S(1)} async-done(((f32[2,2,128,768]{3,0,1,2:T(2,128)}), f32[2,2,128,768]{3,0,1,2:T(2,128)S(1)}, u32[]{:S(2)}, u32[]{:S(2)}) %all-to-all-start.4) | async-done | bytes 1572896 | tf_op jit(solution)/shard_map/all_to_all | solution.py:115
  283.8 9.2 %all-to-all-start.6 = ((f32[2,2,128,384]{3,0,1,2:T(2,128)}), f32[2,2,128,384]{3,0,1,2:T(2,128)}, u32[]{:S(2)}, u32[]{:S(2)}) async-start(f32[2,2,128,384]{3,0,1,2:T(2,128)} %copy.109), calls=%async_computation.7 | async-start | bytes 1572864 | tf_op jit(solution)/shard_map/all_to_all | solution.py:115
  297.9 13.8 %all-to-all-done.6 = f32[2,2,128,384]{3,0,1,2:T(2,128)} async-done(((f32[2,2,128,384]{3,0,1,2:T(2,128)}), f32[2,2,128,384]{3,0,1,2:T(2,128)}, u32[]{:S(2)}, u32[]{:S(2)}) %all-to-all-start.6) | async-done | bytes 786464 | tf_op jit(solution)/shard_map/all_to_all | solution.py:115
  311.7 5.5 %all-to-all-start.5 = ((f32[2,16,8,768]{3,2,0,1:T(8,128)}), f32[2,16,8,768]{3,2,0,1:T(8,128)S(1)}, u32[]{:S(2)}, u32[]{:S(2)}) async-start(f32[2,16,8,768]{3,2,0,1:T(8,128)} %copy.105), calls=%async_computation.5 | async-start | bytes 1572864 | tf_op jit(solution)/shard_map/all_to_all | solution.py:118
  317.2 69.0 %psum.15 = f32[1,8,768]{2,1,0:T(8,128)S(1)} all-reduce(f32[1,8,768]{2,1,0:T(8,128)S(1)} %bitcast.242), channel_id=1, replica_groups=mesh['ctx'=2,'inner'=16] {'inner'}, use_global_device_ids=true, to_apply=%region_7.8 | all-reduce | flops 6144 | bytes 49152 | tf_op jit(solution)/shard_map/psum | solution.py:51
  386.2 4.5 %all_gather.28 = f32[2,8,768]{2,1,0:T(8,128)S(1)} all-gather(f32[1,8,768]{2,1,0:T(8,128)S(1)} %psum.15), channel_id=1, replica_groups=mesh['ctx'=2,'inner'=16] {'ctx'}, dimensions={0}, use_global_device_ids=true | all-gather | bytes 73728 | tf_op jit(solution)/shard_map/all_gather | solution.py:15
  399.6 7.3 %all-to-all-done.7 = f32[1,16,8,384]{3,2,0,1:T(8,128)S(1)} async-done(((f32[1,16,8,384]{3,2,0,1:T(8,128)}), f32[1,16,8,384]{3,2,0,1:T(8,128)S(1)}, u32[]{:S(2)}, u32[]{:S(2)}) %all-to-all-start.7) | async-done | bytes 196640 | tf_op jit(solution)/shard_map/all_to_all | solution.py:118
  406.9 6.8 %all_gather.29 = f32[128,768]{1,0:T(8,128)S(1)} all-gather(f32[128,384]{1,0:T(8,128)S(1)} %bitcast.241), channel_id=1, replica_groups=mesh['ctx'=2,'inner'=16] {'ctx'}, dimensions={1}, use_global_device_ids=true | all-gather | bytes 589824 | tf_op jit(solution)/shard_map/all_gather | solution.py:174
  (105 shorter events, 65.6 us)
Async XLA Ops:
  7.2 2.5 copy-start.12
  7.2 2.5 copy-start.13
  7.2 73.3 %copy-start.5 = (f32[128,768]{1,0:T(8,128)S(1)}, f32[128,768]{1,0:T(8,128)}, u32[]{:S(2)}) copy-start(f32[128,768]{1,0:T(8,128)} %param.11) | copy-start | bytes 1179652
  7.2 73.3 %copy-start.3 = (f32[128,768]{1,0:T(8,128)S(1)}, f32[128,768]{1,0:T(8,128)}, u32[]{:S(2)}) copy-start(f32[128,768]{1,0:T(8,128)} %param.17) | copy-start | bytes 1179652
  8.1 72.5 %copy-start.14 = (f32[8,768]{1,0:T(8,128)S(1)}, f32[8,768]{1,0:T(8,128)}, u32[]{:S(2)}) copy-start(f32[8,768]{1,0:T(8,128)} %param.15) | copy-start | bytes 73732
  80.6 2.2 copy-start.11
  82.8 5.0 %copy-start.10 = (f32[128,768]{1,0:T(8,128)S(1)}, f32[128,768]{1,0:T(8,128)}, u32[]{:S(2)}) copy-start(f32[128,768]{1,0:T(8,128)} %param.12) | copy-start | bytes 1179652
  84.0 15.7 %all-to-all-start = ((f32[1,1,128,768]{3,1,0,2:T(1,128)}), f32[1,1,128,768]{3,1,0,2:T(1,128)S(1)}, u32[]{:S(2)}, u32[]{:S(2)}) async-start(f32[1,1,128,768]{3,1,0,2:T(1,128)} %copy.88), calls=%async_computation | async-start | bytes 786432 | tf_op jit(solution)/shard_map/all_to_all | solution.py:93
  99.7 22.3 %all-to-all-start.2 = ((f32[2,1,128,768]{3,0,1,2:T(2,128)}), f32[2,1,128,768]{3,0,1,2:T(2,128)S(1)}, u32[]{:S(2)}, u32[]{:S(2)}) async-start(f32[2,1,128,768]{3,0,1,2:T(2,128)} %maximum_bitcast_fusion.1), calls=%async_computation.2 | async-start | bytes 1572864 | tf_op jit(solution)/shard_map/all_to_all | solution.py:93
  127.6 5.6 %copy-start.1 = (f32[1,32,8,768]{3,1,2,0:T(8,128)S(1)}, f32[1,32,8,768]{3,1,2,0:T(8,128)}, u32[]{:S(2)}) copy-start(f32[1,32,8,768]{3,1,2,0:T(8,128)} %get-tuple-element.165) | copy-start | bytes 2359300
  127.6 5.6 %copy-start.2 = (f32[1,32,8,768]{3,1,2,0:T(8,128)S(1)}, f32[1,32,8,768]{3,1,2,0:T(8,128)}, u32[]{:S(2)}) copy-start(f32[1,32,8,768]{3,1,2,0:T(8,128)} %get-tuple-element.166) | copy-start | bytes 2359300
  127.6 37.5 %all-to-all-start.3 = ((f32[2,32,8,768]{3,2,0,1:T(8,128)}), f32[2,32,8,768]{3,2,0,1:T(8,128)S(1)}, u32[]{:S(2)}, u32[]{:S(2)}) async-start(f32[2,32,8,768]{3,2,0,1:T(8,128)} %copy.98), calls=%async_computation.3 | async-start | bytes 3145728 | tf_op jit(solution)/shard_map/all_to_all | solution.py:103
  165.2 41.2 %all-to-all-start.1 = ((f32[2,32,8,768]{3,2,0,1:T(8,128)}), f32[2,32,8,768]{3,2,0,1:T(8,128)}, u32[]{:S(2)}, u32[]{:S(2)}) async-start(f32[2,32,8,768]{3,2,0,1:T(8,128)} %copy.90), calls=%async_computation.1 | async-start | bytes 3145728 | tf_op jit(solution)/shard_map/all_to_all | solution.py:103
  174.3 94.9 %reduce-scatter.2.cloned.1.call-start = ((), (), s32[]{:S(2)}) async-start(), calls=%async_computation.9 | async-start | bytes 2359296 | tf_op jit(solution)/shard_map/reduce_scatter | solution.py:172
  175.1 2.7 copy-start.7
  175.2 2.7 copy-start.8
  234.1 2.2 copy-start
  242.2 41.6 %all-to-all-start.4 = ((f32[2,2,128,768]{3,0,1,2:T(2,128)}), f32[2,2,128,768]{3,0,1,2:T(2,128)S(1)}, u32[]{:S(2)}, u32[]{:S(2)}) async-start(f32[2,2,128,768]{3,0,1,2:T(2,128)} %copy.102), calls=%async_computation.4 | async-start | bytes 3145728 | tf_op jit(solution)/shard_map/all_to_all | solution.py:115
  283.8 27.9 %all-to-all-start.6 = ((f32[2,2,128,384]{3,0,1,2:T(2,128)}), f32[2,2,128,384]{3,0,1,2:T(2,128)}, u32[]{:S(2)}, u32[]{:S(2)}) async-start(f32[2,2,128,384]{3,0,1,2:T(2,128)} %copy.109), calls=%async_computation.7 | async-start | bytes 1572864 | tf_op jit(solution)/shard_map/all_to_all | solution.py:115
  311.7 82.7 %all-to-all-start.5 = ((f32[2,16,8,768]{3,2,0,1:T(8,128)}), f32[2,16,8,768]{3,2,0,1:T(8,128)S(1)}, u32[]{:S(2)}, u32[]{:S(2)}) async-start(f32[2,16,8,768]{3,2,0,1:T(8,128)} %copy.105), calls=%async_computation.5 | async-start | bytes 1572864 | tf_op jit(solution)/shard_map/all_to_all | solution.py:118
  393.1 5.4 %copy-start.4 = (f32[128,768]{1,0:T(8,128)S(1)}, f32[128,768]{1,0:T(8,128)}, u32[]{:S(2)}) copy-start(f32[128,768]{1,0:T(8,128)} %param.17) | copy-start | bytes 1179652
  393.1 5.4 %copy-start.6 = (f32[128,768]{1,0:T(8,128)S(1)}, f32[128,768]{1,0:T(8,128)}, u32[]{:S(2)}) copy-start(f32[128,768]{1,0:T(8,128)} %param.11) | copy-start | bytes 1179652
  393.1 5.4 %copy-start.9 = (f32[128,768]{1,0:T(8,128)S(1)}, f32[128,768]{1,0:T(8,128)}, u32[]{:S(2)}) copy-start(f32[128,768]{1,0:T(8,128)} %get-tuple-element.135) | copy-start | bytes 1179652
  394.4 12.5 %all-to-all-start.7 = ((f32[1,16,8,384]{3,2,0,1:T(8,128)}), f32[1,16,8,384]{3,2,0,1:T(8,128)S(1)}, u32[]{:S(2)}, u32[]{:S(2)}) async-start(f32[1,16,8,384]{3,2,0,1:T(8,128)} %copy.112), calls=%async_computation.8 | async-start | bytes 393216 | tf_op jit(solution)/shard_map/all_to_all | solution.py:118
Sparse Core Ops, SparseCore 0:
  238.2 30.9 reduce-scatter.1
where the time goes:
time: 424 us; the launch traced here: 421 us
  blocking collectives  151 us (36%)
  waiting for transfers between devices  123 us (29%)
  local copies, waits for them, and re-layouts  51 us (12%)
  starting transfers between devices  49.8 us (12%)
  other arithmetic  16 us (4%)
  matrix products  15.9 us (4%)
  between operations  14.6 us (3%)
    psum x2, blocking collectives, carried_mode_state(): summed_total = lax.psum(partial_terms, 'inner')  130 us
    all_to_all x2, waiting for transfers between devices, to_spectrum(): lax.all_to_all(turned, 'inner', split_axis=1, concat_axis=2, tiled=True)  46.2 us
    all_to_all x2, waiting for transfers between devices, to_spectrum(): lax.all_to_all(stacked, 'inner', split_axis=2, concat_axis=1, tiled=True)  26.9 us
    all_to_all x2, waiting for transfers between devices, from_spectrum(): lax.all_to_all(turned, 'inner', split_axis=2, concat_axis=1, tiled=True)  25 us
    all_to_all x2, starting transfers between devices, from_spectrum(): lax.all_to_all(turned, 'inner', split_axis=2, concat_axis=1, tiled=True)  18.7 us
    reduce_scatter x1, waiting for transfers between devices, shards(): share_spec = lax.psum_scatter(corr, 'ctx', scatter_dimension=3, tiled=True)  17.4 us
    slice x4, local copies, waits for them, and re-layouts, mirror_rows(): rolled = jnp.roll(flipped, 1, axis=1)  16.7 us
    dot_general x8, matrix products, contract(): return jnp.einsum(form, table, data, precision=FULL_PRECISION)  15.9 us
  transfers between devices with their start and end apart: 9, of which 8 were waited for; matrix products, arithmetic and copies ran while one was open for 9% of the time, Pallas kernels for 0%

commit v1 on v0

--- a/solution.py
+++ b/solution.py
@@ -1,8 +1,12 @@
+import functools
 import math
 
 import jax
 import jax.numpy as jnp
+import numpy as np
 from jax import lax
+from jax.experimental import pallas as pl
+from jax.experimental.pallas import tpu as pltpu
 from jax.sharding import PartitionSpec as P
 
 FULL_PRECISION = lax.Precision.HIGHEST
@@ -176,6 +180,501 @@
     return (mixed_out, grad_gate, grad_value, grad_filter * grad_scale)
 
 
+LANES = 128
+SUBLANES = 8
+
+
+def plus(x, y):
+    return tuple(q if p is None else p if q is None else p + q for p, q in zip(x, y))
+
+
+def minus(x, y):
+    return tuple(
+        p if q is None else -q if p is None else p - q for p, q in zip(x, y)
+    )
+
+
+def scaled(part, factor):
+    if part is None or abs(factor) < 1e-12:
+        return None
+    if abs(factor - 1.0) < 1e-12:
+        return part
+    if abs(factor + 1.0) < 1e-12:
+        return -part
+    return part * factor
+
+
+def turned(x, angle):
+    c, s = math.cos(angle), math.sin(angle)
+    real = minus((scaled(x[0], c),), (scaled(x[1], s),))[0] if x[1] is not None else scaled(x[0], c)
+    imag = plus((scaled(x[0], s),), (scaled(x[1], c),))[0]
+    return (real, imag)
+
+
+def transform_ahead(xs):
+    n = len(xs)
+    if n == 1:
+        return xs
+    h = n // 2
+    total = [plus(xs[i], xs[i + h]) for i in range(h)]
+    apart = [turned(minus(xs[i], xs[i + h]), -2.0 * math.pi * i / n) for i in range(h)]
+    even, odd = transform_ahead(total), transform_ahead(apart)
+    return [(even, odd)[k % 2][k // 2] for k in range(n)]
+
+
+def transform_behind(xs):
+    n = len(xs)
+    if n == 1:
+        return xs
+    h = n // 2
+    even, odd = transform_behind(xs[0::2]), transform_behind(xs[1::2])
+    odd = [turned(odd[i], 2.0 * math.pi * i / n) for i in range(h)]
+    return [plus(even[i], odd[i]) for i in range(h)] + [minus(even[i], odd[i]) for i in range(h)]
+
+
+def split_table(table):
+    high = table.astype(jnp.bfloat16)
+    return high, (table - high.astype(np.float32)).astype(jnp.bfloat16)
+
+
+def line_tables(width, row_count, half):
+    turn = 2.0 * np.pi / width * (np.outer(np.arange(width), np.arange(width)) % width)
+    c, s = np.cos(turn), np.sin(turn)
+    ahead = np.block([[c, -s], [s, c]]).astype(np.float32)
+    behind = np.block([[c, s], [-s, c]]).astype(np.float32)
+    length = width * row_count
+    phase = 2.0 * np.pi / length * np.outer(np.arange(half), np.arange(width))
+    weight = np.full((half, 1), 2.0)
+    weight[0] = weight[-1] = 1.0
+    twist = np.stack(
+        [np.cos(phase), np.sin(phase), np.cos(phase) * weight / length, np.sin(phase) * weight / length]
+    ).astype(np.float32)
+    return split_table(ahead) + split_table(behind) + (twist,)
+
+
+def mixer_kernel(
+    ctx_count,
+    inner_count,
+    modes,
+    gate,
+    value,
+    taps,
+    rate,
+    coeff,
+    keep,
+    cot,
+    ahead_high,
+    ahead_low,
+    behind_high,
+    behind_low,
+    twist,
+    mixed_out,
+    grad_gate,
+    grad_value,
+    grad_filter,
+    send_taps,
+    send_value,
+    send_grad,
+    got_taps,
+    got_value,
+    got_grad,
+    spec,
+    params,
+    out_mix,
+    out_through,
+    out_corr,
+    back_mix,
+    back_through,
+    back_corr,
+    send_sems,
+    recv_sems,
+):
+    n = ctx_count * inner_count
+    width = value.shape[0]
+    chans = send_value.shape[1]
+    chunks = chans // SUBLANES
+    row_count = 2 * inner_count
+    half = inner_count + 1
+    group_len = width * inner_count
+    ctx_idx = lax.axis_index("ctx")
+    inner_idx = lax.axis_index("inner")
+    me = ctx_idx * inner_count + inner_idx
+
+    barrier = pltpu.get_barrier_semaphore()
+
+    def greet(k, carry):
+        d = lax.rem(me + k, n)
+        pl.semaphore_signal(
+            barrier,
+            inc=1,
+            device_id=(lax.div(d, inner_count), lax.rem(d, inner_count)),
+            device_id_type=pl.DeviceIdType.MESH,
+        )
+        return carry
+
+    lax.fori_loop(1, n, greet, 0)
+
+    def copy_to(src, dst, kind, d, source):
+        return pltpu.make_async_remote_copy(
+            src_ref=src,
+            dst_ref=dst,
+            send_sem=send_sems.at[kind, d],
+            recv_sem=recv_sems.at[kind, source],
+            device_id=(lax.div(d, inner_count), lax.rem(d, inner_count)),
+            device_id_type=pl.DeviceIdType.MESH,
+        )
+
+    def everyone(src, dst, kind, fold=False):
+        def piece(k, landing):
+            d = lax.rem(me + k, n)
+            row = lax.rem(d, inner_count) if fold else d
+            return copy_to(src.at[row], dst.at[landing], kind, d, landing)
+
+        def start(k, carry):
+            piece(k, me).start()
+            return carry
+
+        def arrive(k, carry):
+            piece(k, lax.rem(me + n - k, n)).wait_recv()
+            return carry
+
+        def leave(k, carry):
+            piece(k, me).wait_send()
+            return carry
+
+        return tuple(
+            functools.partial(lax.fori_loop, 1, n, step, 0) for step in (start, arrive, leave)
+        )
+
+    def own_group(src, dst, kind):
+        def piece(k, landing):
+            d = ctx_idx * inner_count + lax.rem(inner_idx + k, inner_count)
+            return copy_to(src.at[d], dst.at[landing], kind, d, landing)
+
+        def start(k, carry):
+            piece(k, inner_idx).start()
+            return carry
+
+        def arrive(k, carry):
+            piece(k, lax.rem(inner_idx + inner_count - k, inner_count)).wait_recv()
+            return carry
+
+        def leave(k, carry):
+            piece(k, inner_idx).wait_send()
+            return carry
+
+        return tuple(
+            functools.partial(lax.fori_loop, 1, inner_count, step, 0)
+            for step in (start, arrive, leave)
+        )
+
+    taps_start, taps_arrive, taps_leave = own_group(send_taps, got_taps, 0)
+    value_start, value_arrive, value_leave = everyone(send_value, got_value, 1)
+    grad_start, grad_arrive, grad_leave = everyone(send_grad, got_grad, 2)
+    corr_start, corr_arrive, corr_leave = everyone(out_corr, back_corr, 3, True)
+    mix_start, mix_arrive, mix_leave = everyone(out_mix, back_mix, 4)
+    through_start, through_arrive, through_leave = everyone(out_through, back_through, 5)
+
+    def by_channel(block):
+        return jnp.transpose(block).reshape(n, chans, width)
+
+    send_taps[...] = by_channel(taps[...])
+    pl.semaphore_wait(barrier, n - 1)
+    taps_start()
+    got_taps[inner_idx] = send_taps[me]
+    send_value[...] = by_channel(value[...])
+    value_start()
+    got_value[me] = send_value[me]
+    send_grad[...] = by_channel(cot[...] * gate[...])
+    grad_start()
+    got_grad[me] = send_grad[me]
+
+    rows = [rate[...], coeff[...], keep[...]]
+    filled = sum(r.shape[0] for r in rows)
+    rows.append(jnp.zeros((LANES - filled, rate.shape[1]), jnp.float32))
+    params[...] = jnp.transpose(jnp.concatenate(rows, 0))
+    spec[:, half] = jnp.zeros(spec.shape[:1] + spec.shape[2:], jnp.float32)
+
+    lane = lax.broadcasted_iota(jnp.int32, (SUBLANES, width), 1).astype(jnp.float32)
+
+    def per_channel(chunk):
+        own = params[pl.ds(pl.multiple_of(me * chans + chunk * SUBLANES, SUBLANES), SUBLANES), :]
+
+        def wide(column):
+            return jnp.broadcast_to(own[:, column : column + 1], (SUBLANES, width))
+
+        rates = [wide(m) for m in range(modes)]
+        coeffs = [wide(modes + m) for m in range(modes)]
+        keeps = [
+            [wide((2 + g) * modes + m) for m in range(modes)] for g in range(ctx_count - 1)
+        ]
+        return rates, coeffs, keeps
+
+    def rows_of(chunk):
+        return pl.ds(pl.multiple_of(chunk * SUBLANES, SUBLANES), SUBLANES)
+
+    def add_tail(chunk, carry):
+        rates, coeffs, _ = per_channel(chunk)
+        steps = [jnp.exp(-r * float(width)) for r in rates]
+        terms = [c * jnp.exp(-r * lane) for r, c in zip(rates, coeffs)]
+        at = rows_of(chunk)
+        for i in range(inner_count):
+            got_taps[i, at, :] = got_taps[i, at, :] + sum(terms[1:], terms[0])
+            terms = [t * s for t, s in zip(terms, steps)]
+        return carry
+
+    def rows_ahead(src, base, slot, chunk):
+        at = rows_of(chunk)
+        blank = (None, None)
+        xs = [(src[base + i, at, :], None) for i in range(inner_count)] + [blank] * inner_count
+        parts = transform_ahead(xs)
+        for k in range(half):
+            real, imag = parts[k]
+            c, s = twist[0, k : k + 1, :], twist[1, k : k + 1, :]
+            if imag is None:
+                first, second = real * c, -(real * s)
+            else:
+                first, second = real * c + imag * s, imag * c - real * s
+            spec[slot, k, at, :width] = first
+            spec[slot, k, at, width:] = second
+
+    def line(slot, high, low):
+        data = spec[slot].reshape((half + 1) * chans, 2 * width)
+        top = data.astype(jnp.bfloat16)
+        rest = (data - top.astype(jnp.float32)).astype(jnp.bfloat16)
+        dot = functools.partial(jnp.dot, preferred_element_type=jnp.float32)
+        result = dot(rest, high[...]) + dot(top, low[...]) + dot(top, high[...])
+        spec[slot] = result.reshape(half + 1, chans, 2 * width)
+
+    def rows_behind(slot, chunk):
+        at = rows_of(chunk)
+        xs = []
+        for k in range(half):
+            real, imag = spec[slot, k, at, :width], spec[slot, k, at, width:]
+            c, s = twist[2, k : k + 1, :], twist[3, k : k + 1, :]
+            xs.append((real * c - imag * s, real * s + imag * c))
+        xs += [(None, None)] * (row_count - half)
+        return [y[0] for y in transform_behind(xs)[:inner_count]]
+
+    def to_spectra(src, first_slot, groups):
+        def one(step, carry):
+            g = lax.div(step, chunks)
+            rows_ahead(src, g * inner_count, first_slot + g, lax.rem(step, chunks))
+            return carry
+
+        lax.fori_loop(0, groups * chunks, one, 0)
+
+        def transform(g, carry):
+            line(first_slot + g, ahead_high, ahead_low)
+            return carry
+
+        lax.fori_loop(0, groups, transform, 0)
+
+    taps_arrive()
+    lax.fori_loop(0, chunks, add_tail, 0)
+    kern_slot, value_slot, grad_slot = 0, 1, 1 + ctx_count
+    to_spectra(got_taps, kern_slot, 1)
+    value_arrive()
+    to_spectra(got_value, value_slot, ctx_count)
+    grad_arrive()
+    to_spectra(got_grad, grad_slot, ctx_count)
+
+    def multiply(step, carry):
+        k = lax.div(step, chunks)
+        at = rows_of(lax.rem(step, chunks))
+
+        def load(slot):
+            return spec[slot, k, at, :width], spec[slot, k, at, width:]
+
+        def store(slot, real, imag):
+            spec[slot, k, at, :width] = real
+            spec[slot, k, at, width:] = imag
+
+        kr, ki = load(kern_slot)
+        corr_r = corr_i = 0.0
+        for g in range(ctx_count):
+            vr, vi = load(value_slot + g)
+            gr, gi = load(grad_slot + g)
+            corr_r = corr_r + (vr * gr + vi * gi)
+            corr_i = corr_i + (vr * gi - vi * gr)
+            store(value_slot + g, kr * vr - ki * vi, kr * vi + ki * vr)
+            store(grad_slot + g, kr * gr + ki * gi, kr * gi - ki * gr)
+        store(kern_slot, corr_r, corr_i)
+        return carry
+
+    lax.fori_loop(0, half * chunks, multiply, 0)
+
+    grad_scale = 1.0 / math.sqrt(group_len * ctx_count)
+    line(kern_slot, behind_high, behind_low)
+
+    def corr_rows(chunk, carry):
+        for i, y in enumerate(rows_behind(kern_slot, chunk)):
+            out_corr[i, rows_of(chunk), :] = y * grad_scale
+        return carry
+
+    lax.fori_loop(0, chunks, corr_rows, 0)
+    corr_start()
+    back_corr[me] = out_corr[inner_idx]
+
+    def from_spectra(first_slot, dst):
+        def transform(g, carry):
+            line(first_slot + g, behind_high, behind_low)
+            return carry
+
+        lax.fori_loop(0, ctx_count, transform, 0)
+
+        def one(step, carry):
+            g, chunk = lax.div(step, chunks), lax.rem(step, chunks)
+            for i, y in enumerate(rows_behind(first_slot + g, chunk)):
+                dst[g * inner_count + i, rows_of(chunk), :] = y
+            return carry
+
+        lax.fori_loop(0, ctx_count * chunks, one, 0)
+
+    def carried_ahead(chunk, carry):
+        rates, coeffs, keeps = per_channel(chunk)
+        at = rows_of(chunk)
+        steps = [jnp.exp(-r * float(width)) for r in rates]
+        whole = [jnp.exp(-r * float(group_len)) for r in rates]
+        to_end = [jnp.exp(-r * (width - 1.0 - lane)) for r in rates]
+        from_start = [c * jnp.exp(-r * (lane + 1.0)) for r, c in zip(rates, coeffs)]
+        state = [jnp.zeros((SUBLANES, 1), jnp.float32)] * modes
+        for g in range(ctx_count - 1):
+            acc = [jnp.zeros((SUBLANES, width), jnp.float32)] * modes
+            for i in range(inner_count):
+                block = got_value[g * inner_count + i, at, :]
+                acc = [a * s + block for a, s in zip(acc, steps)]
+            for m in range(modes):
+                total = jnp.sum(acc[m] * to_end[m], 1, keepdims=True)
+                state[m] = keeps[g][m][:, :1] * (whole[m][:, :1] * state[m] + total)
+            terms = [f * st for f, st in zip(from_start, state)]
+            for i in range(inner_count):
+                row = (g + 1) * inner_count + i
+                out_mix[row, at, :] = out_mix[row, at, :] + sum(terms[1:], terms[0])
+                terms = [t * s for t, s in zip(terms, steps)]
+        return carry
+
+    def carried_behind(chunk, carry):
+        rates, coeffs, keeps = per_channel(chunk)
+        at = rows_of(chunk)
+        steps = [jnp.exp(-r * float(width)) for r in rates]
+        whole = [jnp.exp(-r * float(group_len)) for r in rates]
+        to_end = [jnp.exp(-r * (width - 1.0 - lane)) for r in rates]
+        from_start = [c * jnp.exp(-r * (lane + 1.0)) for r, c in zip(rates, coeffs)]
+        state = [jnp.zeros((SUBLANES, 1), jnp.float32)] * modes
+        for g in reversed(range(1, ctx_count)):
+            acc = [jnp.zeros((SUBLANES, width), jnp.float32)] * modes
+            for i in reversed(range(inner_count)):
+                block = got_grad[g * inner_count + i, at, :]
+                acc = [a * s + block for a, s in zip(acc, steps)]
+            for m in range(modes):
+                total = jnp.sum(acc[m] * from_start[m], 1, keepdims=True)
+                if g < ctx_count - 1:
+                    state[m] = total + whole[m][:, :1] * keeps[g][m][:, :1] * state[m]
+                else:
+                    state[m] = total
+            terms = [
+                t * (kp[:, :1] * st) for t, kp, st in zip(to_end, keeps[g - 1], state)
+            ]
+            for i in reversed(range(inner_count)):
+                row = (g - 1) * inner_count + i
+                out_through[row, at, :] = out_through[row, at, :] + sum(terms[1:], terms[0])
+                terms = [t * s for t, s in zip(terms, steps)]
+        return carry
+
+    from_spectra(value_slot, out_mix)
+    lax.fori_loop(0, chunks, carried_ahead, 0)
+    mix_start()
+    back_mix[me] = out_mix[me]
+    from_spectra(grad_slot, out_through)
+    lax.fori_loop(0, chunks, carried_behind, 0)
+    through_start()
+    back_through[me] = out_through[me]
+
+    def by_token(blocks):
+        return jnp.transpose(blocks[...].reshape(n * chans, width))
+
+    corr_arrive()
+    grad_filter[...] = by_token(back_corr)
+    mix_arrive()
+    mixture = by_token(back_mix)
+    mixed_out[...] = gate[...] * mixture
+    grad_gate[...] = cot[...] * mixture
+    through_arrive()
+    grad_value[...] = by_token(back_through)
+    for leave in (taps_leave, value_leave, grad_leave, corr_leave, mix_leave, through_leave):
+        leave()
+
+
+def fits(mesh, value_input):
+    inner_count, ctx_count = mesh.shape["inner"], mesh.shape["ctx"]
+    tok_dev, channels = value_input.shape
+    return (
+        tok_dev == LANES
+        and channels % (inner_count * ctx_count * SUBLANES) == 0
+        and inner_count & (inner_count - 1) == 0
+    )
+
+
+def shards_by_channel(
+    mesh, gate_input, value_input, filter_taps, decay_rate, mode_coeff, boundary_keep, cotangent
+):
+    inner_count, ctx_count = mesh.shape["inner"], mesh.shape["ctx"]
+    n = inner_count * ctx_count
+    tok_dev, channels = value_input.shape
+    modes = decay_rate.shape[0]
+    chans = channels // n
+    half = inner_count + 1
+    tables = line_tables(tok_dev, 2 * inner_count, half)
+    keep_rows = boundary_keep.reshape(-1, channels)
+    block = jax.ShapeDtypeStruct((tok_dev, channels), jnp.float32)
+    f32 = functools.partial(pltpu.VMEM, dtype=jnp.float32)
+    pieces, own_pieces = f32((n, chans, tok_dev)), f32((inner_count, chans, tok_dev))
+    vmem = pl.BlockSpec(memory_space=pltpu.VMEM)
+    return pl.pallas_call(
+        functools.partial(mixer_kernel, ctx_count, inner_count, modes),
+        out_shape=(block,) * 4,
+        in_specs=[vmem] * 12,
+        out_specs=(vmem,) * 4,
+        scratch_shapes=[
+            pieces,
+            pieces,
+            pieces,
+            own_pieces,
+            pieces,
+            pieces,
+            f32((1 + 2 * ctx_count, half + 1, chans, 2 * tok_dev)),
+            f32((channels, LANES)),
+            pieces,
+            pieces,
+            own_pieces,
+            pieces,
+            pieces,
+            pieces,
+            pltpu.SemaphoreType.DMA((6, n)),
+            pltpu.SemaphoreType.DMA((6, n)),
+        ],
+        compiler_params=pltpu.CompilerParams(
+            collective_id=0, has_side_effects=True, vmem_limit_bytes=40 * 1024 * 1024
+        ),
+    )(
+        gate_input,
+        value_input,
+        filter_taps,
+        decay_rate,
+        mode_coeff,
+        keep_rows,
+        cotangent,
+        *tables,
+    )
+
+
+def shards_of(mesh, *args):
+    if fits(mesh, args[1]):
+        return shards_by_channel(mesh, *args)
+    return shards(*args)
+
+
 def solution(mesh):
     placed = (
         P(("ctx", "inner"), None),
@@ -187,7 +686,7 @@
         P(("ctx", "inner"), None),
     )
     return jax.shard_map(
-        shards,
+        functools.partial(shards_of, mesh),
         mesh=mesh,
         in_specs=placed,
         out_specs=(

time: 424 us -> 79.1 us (0.19)
  blocking collectives: 151 us -> 0 us
  waiting for transfers between devices: 123 us -> 0 us
  Pallas kernels: 0 us -> 64.3 us
  starting transfers between devices: 49.8 us -> 0 us
  local copies, waits for them, and re-layouts: 51 us -> 13.6 us
  other arithmetic: 16 us -> 0 us
  matrix products: 15.9 us -> 0 us
  between operations: 14.6 us -> 0.66 us
    psum x2 -> x0, blocking collectives: 130 us -> none  [carried_mode_state(): summed_total = lax.psum(partial_terms, 'inner')]
    all_to_all x8 -> x0, waiting for transfers between devices: 105 us -> none  [the longest x2 46.2 us: to_spectrum(): lax.all_to_all(turned, 'inner', split_axis=1, concat_axis=2, tiled=True)]
    pallas_call x0 -> x1, Pallas kernels: none -> 64.3 us  [shards_by_channel(): pl.pallas_call(functools.partial(mixer_kernel, ctx_count, inner_count, mo...]
    all_to_all x8 -> x0, starting transfers between devices: 49.6 us -> none  [the longest x2 18.7 us: from_spectrum(): lax.all_to_all(turned, 'inner', split_axis=2, concat_axis=1, tiled=True)]
    slice x7 -> x0, local copies, waits for them, and re-layouts: 25.7 us -> none  [the longest x4 16.7 us: mirror_rows(): rolled = jnp.roll(flipped, 1, axis=1)]
    all_gather x4 -> x0, blocking collectives: 21.2 us -> none  [the longest x3 14.4 us: prefix(): gathered = jax.tree.map(lambda a: lax.all_gather(a, axis), part)]
    reduce_scatter x1 -> x0, waiting for transfers between devices: 17.4 us -> none  [shards(): share_spec = lax.psum_scatter(corr, 'ctx', scatter_dimension=3, tiled=True)]
    dot_general x8 -> x0, matrix products: 15.9 us -> none  [contract(): return jnp.einsum(form, table, data, precision=FULL_PRECISION)]
  transfers between devices with their start and end apart: 9 -> 0, of which waited for: 8 -> 0; matrix products, arithmetic and copies ran while one was open for 9% -> 0% of each run, Pallas kernels for 0% -> 0%
where the time goes in v1:
time: 79.1 us; the launch traced here: 78.5 us
  Pallas kernels  64.3 us (81%)
  local copies, waits for them, and re-layouts  13.6 us (17%)
    pallas_call x1, Pallas kernels, shards_by_channel(): pl.pallas_call(functools.partial(mixer_kernel, ctx_count, inner_count, mo...  64.3 us
    unnamed x28, local copies, waits for them, and re-layouts  13.6 us

profile of v1, /device:TPU:0, one launch (start us, length us, event | category | flops | bytes accessed | tf_op | source)
XLA Modules:
  0.0 78.5 jit_solution(13706265657762046284)
XLA Ops:
  0.6 0.0 copy-start
  0.6 1.0 %copy-done = f32[128,768]{1,0:T(8,128)S(1)} copy-done((f32[128,768]{1,0:T(8,128)S(1)}, f32[128,768]{1,0:T(8,128)}, u32[]{:S(2)}) %copy-start) | copy-done | bytes 393240
  1.6 0.0 copy-start.1
  1.6 1.0 %copy-done.1 = f32[128,768]{1,0:T(8,128)S(1)} copy-done((f32[128,768]{1,0:T(8,128)S(1)}, f32[128,768]{1,0:T(8,128)}, u32[]{:S(2)}) %copy-start.1) | copy-done | bytes 393240
  2.6 0.0 copy-start.2
  2.6 1.0 %copy-done.2 = f32[128,768]{1,0:T(8,128)S(1)} copy-done((f32[128,768]{1,0:T(8,128)S(1)}, f32[128,768]{1,0:T(8,128)}, u32[]{:S(2)}) %copy-start.2) | copy-done | bytes 393240
  3.6 0.0 copy-start.3
  3.6 1.0 %copy-done.3 = f32[128,768]{1,0:T(8,128)S(1)} copy-done((f32[128,768]{1,0:T(8,128)S(1)}, f32[128,768]{1,0:T(8,128)}, u32[]{:S(2)}) %copy-start.3) | copy-done | bytes 393240
  4.6 0.0 copy-start.4
  4.6 0.9 %copy-done.4 = bf16[256,256]{1,0:T(8,128)(2,1)S(1)} copy-done((bf16[256,256]{1,0:T(8,128)(2,1)S(1)}, bf16[256,256]{1,0:T(8,128)(2,1)}, u32[]{:S(2)}) %copy-start.4) | copy-done | bytes 131096
  5.5 0.0 copy-start.5
  5.5 0.9 %copy-done.5 = bf16[256,256]{1,0:T(8,128)(2,1)S(1)} copy-done((bf16[256,256]{1,0:T(8,128)(2,1)S(1)}, bf16[256,256]{1,0:T(8,128)(2,1)}, u32[]{:S(2)}) %copy-start.5) | copy-done | bytes 131096
  6.4 0.0 copy-start.6
  6.4 0.9 %copy-done.6 = bf16[256,256]{1,0:T(8,128)(2,1)S(1)} copy-done((bf16[256,256]{1,0:T(8,128)(2,1)S(1)}, bf16[256,256]{1,0:T(8,128)(2,1)}, u32[]{:S(2)}) %copy-start.6) | copy-done | bytes 131096
  7.3 0.9 %copy-done.7 = bf16[256,256]{1,0:T(8,128)(2,1)S(1)} copy-done((bf16[256,256]{1,0:T(8,128)(2,1)S(1)}, bf16[256,256]{1,0:T(8,128)(2,1)}, u32[]{:S(2)}) %copy-start.7) | copy-done | bytes 131096
  8.2 0.8 %copy-done.8 = f32[4,17,128]{2,1,0:T(8,128)S(1)} copy-done((f32[4,17,128]{2,1,0:T(8,128)S(1)}, f32[4,17,128]{2,1,0:T(8,128)}, u32[]{:S(2)}) %copy-start.8) | copy-done | bytes 34840
  9.0 0.7 copy-done.9
  9.8 0.7 copy-done.10
  10.5 0.7 copy-done.11
  11.3 64.3 %shard_map.147 = (f32[128,768]{1,0:T(8,128)S(1)}, f32[128,768]{1,0:T(8,128)S(1)}, f32[128,768]{1,0:T(8,128)S(1)}, f32[128,768]{1,0:T(8,128)S(1)}) custom-call(f32[128,768]{1,0:T(8,128)S(1)} %copy-done, f32[128,768]{1,0:T(8,128)S(1)} %copy-done.1, f32[128,768]{1,0:T(8,128)S(1)} %copy-done.2, f32[8,768]{1,0:T(8,128)S(1)} %copy-done.9, ...), custom_call_target="tpu_custom_call" | custom-call | tf_op jit(solution)/shard_map/pallas_call | solution.py:634
  75.5 0.7 copy.20
  76.3 0.7 copy.21
  77.0 0.7 copy.22
  77.8 0.7 copy.23
  (5 shorter events, 0.0 us)
Async XLA Ops:
  0.6 1.0 %copy-start = (f32[128,768]{1,0:T(8,128)S(1)}, f32[128,768]{1,0:T(8,128)}, u32[]{:S(2)}) copy-start(f32[128,768]{1,0:T(8,128)} %gate.1) | copy-start | bytes 1179652
  1.6 1.0 %copy-start.1 = (f32[128,768]{1,0:T(8,128)S(1)}, f32[128,768]{1,0:T(8,128)}, u32[]{:S(2)}) copy-start(f32[128,768]{1,0:T(8,128)} %value.1) | copy-start | bytes 1179652
  2.6 1.0 %copy-start.2 = (f32[128,768]{1,0:T(8,128)S(1)}, f32[128,768]{1,0:T(8,128)}, u32[]{:S(2)}) copy-start(f32[128,768]{1,0:T(8,128)} %taps.1) | copy-start | bytes 1179652
  3.6 1.0 %copy-start.3 = (f32[128,768]{1,0:T(8,128)S(1)}, f32[128,768]{1,0:T(8,128)}, u32[]{:S(2)}) copy-start(f32[128,768]{1,0:T(8,128)} %cot.1) | copy-start | bytes 1179652
  4.6 0.9 %copy-start.4 = (bf16[256,256]{1,0:T(8,128)(2,1)S(1)}, bf16[256,256]{1,0:T(8,128)(2,1)}, u32[]{:S(2)}) copy-start(bf16[256,256]{1,0:T(8,128)(2,1)} %constant.13.clone.behind_low) | copy-start | bytes 393220
  5.5 0.9 %copy-start.5 = (bf16[256,256]{1,0:T(8,128)(2,1)S(1)}, bf16[256,256]{1,0:T(8,128)(2,1)}, u32[]{:S(2)}) copy-start(bf16[256,256]{1,0:T(8,128)(2,1)} %constant.12.clone.behind_high) | copy-start | bytes 393220
  6.4 0.9 %copy-start.6 = (bf16[256,256]{1,0:T(8,128)(2,1)S(1)}, bf16[256,256]{1,0:T(8,128)(2,1)}, u32[]{:S(2)}) copy-start(bf16[256,256]{1,0:T(8,128)(2,1)} %constant.11.clone.ahead_low) | copy-start | bytes 393220
  7.3 0.9 %copy-start.7 = (bf16[256,256]{1,0:T(8,128)(2,1)S(1)}, bf16[256,256]{1,0:T(8,128)(2,1)}, u32[]{:S(2)}) copy-start(bf16[256,256]{1,0:T(8,128)(2,1)} %constant.10.clone.ahead_high) | copy-start | bytes 393220
  8.2 0.8 %copy-start.8 = (f32[4,17,128]{2,1,0:T(8,128)S(1)}, f32[4,17,128]{2,1,0:T(8,128)}, u32[]{:S(2)}) copy-start(f32[4,17,128]{2,1,0:T(8,128)} %constant.14.clone.twist) | copy-start | bytes 104452
  9.0 0.7 copy-start.9
  9.8 0.7 copy-start.10
  10.5 0.7 copy-start.11

commit v2 on v1

--- a/solution.py
+++ b/solution.py
@@ -232,16 +232,10 @@
     return [plus(even[i], odd[i]) for i in range(h)] + [minus(even[i], odd[i]) for i in range(h)]
 
 
-def split_table(table):
-    high = table.astype(jnp.bfloat16)
-    return high, (table - high.astype(np.float32)).astype(jnp.bfloat16)
-
-
 def line_tables(width, row_count, half):
     turn = 2.0 * np.pi / width * (np.outer(np.arange(width), np.arange(width)) % width)
     c, s = np.cos(turn), np.sin(turn)
-    ahead = np.block([[c, -s], [s, c]]).astype(np.float32)
-    behind = np.block([[c, s], [-s, c]]).astype(np.float32)
+    line = np.concatenate([c, s], 1).astype(np.float32)
     length = width * row_count
     phase = 2.0 * np.pi / length * np.outer(np.arange(half), np.arange(width))
     weight = np.full((half, 1), 2.0)
@@ -249,13 +243,26 @@
     twist = np.stack(
         [np.cos(phase), np.sin(phase), np.cos(phase) * weight / length, np.sin(phase) * weight / length]
     ).astype(np.float32)
-    return split_table(ahead) + split_table(behind) + (twist,)
+    return line, twist
 
 
 def mixer_kernel(
     ctx_count,
     inner_count,
     modes,
+    gate_hbm,
+    value_hbm,
+    taps_hbm,
+    rate_hbm,
+    coeff_hbm,
+    keep_hbm,
+    cot_hbm,
+    circle_hbm,
+    twist_hbm,
+    mixed_hbm,
+    gated_hbm,
+    turned_hbm,
+    filtered_hbm,
     gate,
     value,
     taps,
@@ -263,15 +270,12 @@
     coeff,
     keep,
     cot,
+    circle,
+    twist,
     ahead_high,
     ahead_low,
     behind_high,
     behind_low,
-    twist,
-    mixed_out,
-    grad_gate,
-    grad_value,
-    grad_filter,
     send_taps,
     send_value,
     send_grad,
@@ -286,6 +290,12 @@
     back_mix,
     back_through,
     back_corr,
+    mixed_out,
+    grad_gate,
+    grad_value,
+    grad_filter,
+    load_sems,
+    store_sems,
     send_sems,
     recv_sems,
 ):
@@ -300,6 +310,23 @@
     inner_idx = lax.axis_index("inner")
     me = ctx_idx * inner_count + inner_idx
 
+    pairs = (
+        (taps_hbm, taps),
+        (value_hbm, value),
+        (gate_hbm, gate),
+        (cot_hbm, cot),
+        (rate_hbm, rate),
+        (coeff_hbm, coeff),
+        (keep_hbm, keep),
+        (twist_hbm, twist),
+        (circle_hbm, circle),
+    )
+    loads = [
+        pltpu.make_async_copy(src, dst, load_sems.at[i]) for i, (src, dst) in enumerate(pairs)
+    ]
+    for load in loads:
+        load.start()
+
     barrier = pltpu.get_barrier_semaphore()
 
     def greet(k, carry):
@@ -314,85 +341,89 @@
 
     lax.fori_loop(1, n, greet, 0)
 
-    def copy_to(src, dst, kind, d, source):
+    def copy_to(src, dst, kind, d):
         return pltpu.make_async_remote_copy(
             src_ref=src,
             dst_ref=dst,
-            send_sem=send_sems.at[kind, d],
-            recv_sem=recv_sems.at[kind, source],
+            send_sem=send_sems.at[kind],
+            recv_sem=recv_sems.at[kind],
             device_id=(lax.div(d, inner_count), lax.rem(d, inner_count)),
             device_id_type=pl.DeviceIdType.MESH,
         )
 
-    def everyone(src, dst, kind, fold=False):
-        def piece(k, landing):
+    def exchange(src, dst, kind, partners, copy):
+        def start(k, carry):
+            copy(k).start()
+            return carry
+
+        every = pl.ds(0, partners)
+        whole = copy_to(src.at[every], dst.at[every], kind, lax.rem(me + 1, n))
+        return functools.partial(lax.fori_loop, 1, partners + 1, start, 0), whole
+
+    def everyone(src, dst, kind):
+        def copy(k):
             d = lax.rem(me + k, n)
-            row = lax.rem(d, inner_count) if fold else d
-            return copy_to(src.at[row], dst.at[landing], kind, d, landing)
-
-        def start(k, carry):
-            piece(k, me).start()
-            return carry
-
-        def arrive(k, carry):
-            piece(k, lax.rem(me + n - k, n)).wait_recv()
-            return carry
-
-        def leave(k, carry):
-            piece(k, me).wait_send()
-            return carry
-
-        return tuple(
-            functools.partial(lax.fori_loop, 1, n, step, 0) for step in (start, arrive, leave)
-        )
+            return copy_to(src.at[d], dst.at[me], kind, d)
+
+        return exchange(src, dst, kind, n - 1, copy)
 
     def own_group(src, dst, kind):
-        def piece(k, landing):
+        def copy(k):
             d = ctx_idx * inner_count + lax.rem(inner_idx + k, inner_count)
-            return copy_to(src.at[d], dst.at[landing], kind, d, landing)
-
-        def start(k, carry):
-            piece(k, inner_idx).start()
-            return carry
-
-        def arrive(k, carry):
-            piece(k, lax.rem(inner_idx + inner_count - k, inner_count)).wait_recv()
-            return carry
-
-        def leave(k, carry):
-            piece(k, inner_idx).wait_send()
-            return carry
-
-        return tuple(
-            functools.partial(lax.fori_loop, 1, inner_count, step, 0)
-            for step in (start, arrive, leave)
-        )
-
-    taps_start, taps_arrive, taps_leave = own_group(send_taps, got_taps, 0)
-    value_start, value_arrive, value_leave = everyone(send_value, got_value, 1)
-    grad_start, grad_arrive, grad_leave = everyone(send_grad, got_grad, 2)
-    corr_start, corr_arrive, corr_leave = everyone(out_corr, back_corr, 3, True)
-    mix_start, mix_arrive, mix_leave = everyone(out_mix, back_mix, 4)
-    through_start, through_arrive, through_leave = everyone(out_through, back_through, 5)
+            return copy_to(src.at[d], dst.at[inner_idx], kind, d)
+
+        return exchange(src, dst, kind, inner_count - 1, copy)
+
+    def folded(src, dst, kind):
+        def copy(k):
+            d = lax.rem(me + k, n)
+            return copy_to(src.at[lax.rem(d, inner_count)], dst.at[me], kind, d)
+
+        return exchange(dst, dst, kind, n - 1, copy)
+
+    taps_start, taps_all = own_group(send_taps, got_taps, 0)
+    value_start, value_all = everyone(send_value, got_value, 1)
+    grad_start, grad_all = everyone(send_grad, got_grad, 2)
+    corr_start, corr_all = folded(out_corr, back_corr, 3)
+    mix_start, mix_all = everyone(out_mix, back_mix, 4)
+    through_start, through_all = everyone(out_through, back_through, 5)
 
     def by_channel(block):
         return jnp.transpose(block).reshape(n, chans, width)
 
+    loads[0].wait()
     send_taps[...] = by_channel(taps[...])
     pl.semaphore_wait(barrier, n - 1)
     taps_start()
     got_taps[inner_idx] = send_taps[me]
+    loads[1].wait()
     send_value[...] = by_channel(value[...])
     value_start()
     got_value[me] = send_value[me]
+    loads[2].wait()
+    loads[3].wait()
     send_grad[...] = by_channel(cot[...] * gate[...])
     grad_start()
     got_grad[me] = send_grad[me]
 
+    for load in loads[4:]:
+        load.wait()
     rows = [rate[...], coeff[...], keep[...]]
     filled = sum(r.shape[0] for r in rows)
     rows.append(jnp.zeros((LANES - filled, rate.shape[1]), jnp.float32))
     params[...] = jnp.transpose(jnp.concatenate(rows, 0))
+    cosine, sine = circle[:, :width], circle[:, width:]
+    for high, low, sign in ((ahead_high, ahead_low, 1.0), (behind_high, behind_low, -1.0)):
+        table = jnp.concatenate(
+            [
+                jnp.concatenate([cosine, -sign * sine], 1),
+                jnp.concatenate([sign * sine, cosine], 1),
+            ],
+            0,
+        )
+        top = table.astype(jnp.bfloat16)
+        high[...] = top
+        low[...] = (table - top.astype(jnp.float32)).astype(jnp.bfloat16)
     spec[:, half] = jnp.zeros(spec.shape[:1] + spec.shape[2:], jnp.float32)
 
     lane = lax.broadcasted_iota(jnp.int32, (SUBLANES, width), 1).astype(jnp.float32)
@@ -470,13 +501,13 @@
 
         lax.fori_loop(0, groups, transform, 0)
 
-    taps_arrive()
+    taps_all.wait_recv()
     lax.fori_loop(0, chunks, add_tail, 0)
     kern_slot, value_slot, grad_slot = 0, 1, 1 + ctx_count
     to_spectra(got_taps, kern_slot, 1)
-    value_arrive()
+    value_all.wait_recv()
     to_spectra(got_value, value_slot, ctx_count)
-    grad_arrive()
+    grad_all.wait_recv()
     to_spectra(got_grad, grad_slot, ctx_count)
 
     def multiply(step, carry):
@@ -594,16 +625,49 @@
     def by_token(blocks):
         return jnp.transpose(blocks[...].reshape(n * chans, width))
 
-    corr_arrive()
+    corr_all.wait_recv()
+    stores = [
+        pltpu.make_async_copy(src, dst, store_sems.at[i])
+        for i, (src, dst) in enumerate(
+            (
+                (mixed_out, mixed_hbm),
+                (grad_gate, gated_hbm),
+                (grad_value, turned_hbm),
+                (grad_filter, filtered_hbm),
+            )
+        )
+    ]
     grad_filter[...] = by_token(back_corr)
-    mix_arrive()
+    stores[3].start()
+    mix_all.wait_recv()
     mixture = by_token(back_mix)
     mixed_out[...] = gate[...] * mixture
+    stores[0].start()
     grad_gate[...] = cot[...] * mixture
-    through_arrive()
+    stores[1].start()
+    through_all.wait_recv()
     grad_value[...] = by_token(back_through)
-    for leave in (taps_leave, value_leave, grad_leave, corr_leave, mix_leave, through_leave):
-        leave()
+    stores[2].start()
+    for whole in (taps_all, value_all, grad_all, corr_all, mix_all, through_all):
+        whole.wait_send()
+    for store in stores:
+        store.wait()
+
+
+def finish_kernel(pieces, *refs):
+    sources, targets, sems = refs[:4], refs[4:8], refs[8]
+    rows = sources[0].shape[0] // pieces
+    copies = [
+        pltpu.make_async_copy(
+            src.at[pl.ds(p * rows, rows)], dst.at[pl.ds(p * rows, rows)], sems.at[i, p]
+        )
+        for i, (src, dst) in enumerate(zip(sources, targets))
+        for p in range(pieces)
+    ]
+    for copy in copies:
+        copy.start()
+    for copy in copies:
+        copy.wait()
 
 
 def fits(mesh, value_input):
@@ -630,34 +694,8 @@
     block = jax.ShapeDtypeStruct((tok_dev, channels), jnp.float32)
     f32 = functools.partial(pltpu.VMEM, dtype=jnp.float32)
     pieces, own_pieces = f32((n, chans, tok_dev)), f32((inner_count, chans, tok_dev))
-    vmem = pl.BlockSpec(memory_space=pltpu.VMEM)
-    return pl.pallas_call(
-        functools.partial(mixer_kernel, ctx_count, inner_count, modes),
-        out_shape=(block,) * 4,
-        in_specs=[vmem] * 12,
-        out_specs=(vmem,) * 4,
-        scratch_shapes=[
-            pieces,
-            pieces,
-            pieces,
-            own_pieces,
-            pieces,
-            pieces,
-            f32((1 + 2 * ctx_count, half + 1, chans, 2 * tok_dev)),
-            f32((channels, LANES)),
-            pieces,
-            pieces,
-            own_pieces,
-            pieces,
-            pieces,
-            pieces,
-            pltpu.SemaphoreType.DMA((6, n)),
-            pltpu.SemaphoreType.DMA((6, n)),
-        ],
-        compiler_params=pltpu.CompilerParams(
-            collective_id=0, has_side_effects=True, vmem_limit_bytes=40 * 1024 * 1024
-        ),
-    )(
+    hbm = pl.BlockSpec(memory_space=pltpu.HBM)
+    operands = (
         gate_input,
         value_input,
         filter_taps,
@@ -667,6 +705,48 @@
         cotangent,
         *tables,
     )
+    results = pl.pallas_call(
+        functools.partial(mixer_kernel, ctx_count, inner_count, modes),
+        out_shape=(block,) * 4,
+        in_specs=[hbm] * len(operands),
+        out_specs=(hbm,) * 4,
+        scratch_shapes=[pltpu.VMEM(a.shape, a.dtype) for a in operands]
+        + [pltpu.VMEM((2 * tok_dev, 2 * tok_dev), jnp.bfloat16)] * 4
+        + [
+            pieces,
+            pieces,
+            pieces,
+            own_pieces,
+            pieces,
+            pieces,
+            f32((1 + 2 * ctx_count, half + 1, chans, 2 * tok_dev)),
+            f32((channels, LANES)),
+            pieces,
+            pieces,
+            own_pieces,
+            pieces,
+            pieces,
+            pieces,
+        ]
+        + [f32((tok_dev, channels))] * 4
+        + [
+            pltpu.SemaphoreType.DMA((len(operands),)),
+            pltpu.SemaphoreType.DMA((4,)),
+            pltpu.SemaphoreType.DMA((6,)),
+            pltpu.SemaphoreType.DMA((6,)),
+        ],
+        compiler_params=pltpu.CompilerParams(
+            collective_id=0, has_side_effects=True, vmem_limit_bytes=60 * 1024 * 1024
+        ),
+    )(*operands)
+    return pl.pallas_call(
+        functools.partial(finish_kernel, 2),
+        out_shape=(block,) * 4,
+        in_specs=[hbm] * 4,
+        out_specs=(hbm,) * 4,
+        scratch_shapes=[pltpu.SemaphoreType.DMA((4, 2))],
+        compiler_params=pltpu.CompilerParams(vmem_limit_bytes=60 * 1024 * 1024),
+    )(*results)
 
 
 def shards_of(mesh, *args):

time: 79.1 us -> 110 us (1.39)
  Pallas kernels: 64.3 us -> 109 us
  local copies, waits for them, and re-layouts: 13.6 us -> 0 us
    pallas_call x0 -> x1, Pallas kernels: none -> 48.8 us  [shards_by_channel(): pl.pallas_call(functools.partial(finish_kernel, 2), out_shape=(block,) *...]
    unnamed x28 -> x0, local copies, waits for them, and re-layouts: 13.6 us -> none
    pallas_call x1, Pallas kernels: 64.3 us -> 60.3 us  [shards_by_channel(): pl.pallas_call(functools.partial(mixer_kernel, ctx_count, inner_count, mo...]
where the time goes in v2:
time: 110 us
  Pallas kernels  109 us (99%)
    pallas_call x1, Pallas kernels, shards_by_channel(): pl.pallas_call(functools.partial(mixer_kernel, ctx_count, inner_count, mo...  60.3 us
    pallas_call x1, Pallas kernels, shards_by_channel(): pl.pallas_call(functools.partial(finish_kernel, 2), out_shape=(block,) *...  48.8 us

profile of v2, /device:TPU:0, one launch (start us, length us, event | category | flops | bytes accessed | tf_op | source)
XLA Modules:
  0.0 109.7 jit_solution(1162612379019623223)
XLA Ops:
  0.6 60.3 %shard_map.120 = (f32[128,768]{1,0:T(8,128)}, f32[128,768]{1,0:T(8,128)}, f32[128,768]{1,0:T(8,128)}, f32[128,768]{1,0:T(8,128)}) custom-call(f32[128,768]{1,0:T(8,128)} %gate_hbm.1, f32[128,768]{1,0:T(8,128)} %value_hbm.1, f32[128,768]{1,0:T(8,128)} %taps_hbm.1, f32[8,768]{1,0:T(8,128)} %rate_hbm.1, f32[8,768]{1,0:T(8,128)} %coeff_hbm.1, f32[8,768]{1,0:T(8,128)} %bitcast.1, ...), custom_call_target="tpu_custom_call" | custom-call | tf_op jit(solution)/shard_map/pallas_call | solution.py:708
  60.9 48.8 %shard_map.121 = (f32[128,768]{1,0:T(8,128)}, f32[128,768]{1,0:T(8,128)}, f32[128,768]{1,0:T(8,128)}, f32[128,768]{1,0:T(8,128)}) custom-call(f32[128,768]{1,0:T(8,128)} %get-tuple-element.8.refs_0_, f32[128,768]{1,0:T(8,128)} %get-tuple-element.9.refs_1_, f32[128,768]{1,0:T(8,128)} %get-tuple-element.10.refs_2_, f32[128,768]{1,0:T(8,128)} %get-tuple-element.11.refs_3_), custom_call_target="tpu_custom_call" | custom-call | tf_op jit(solution)/shard_map/pallas_call | solution.py:742

commit v3 on v2

--- a/solution.py
+++ b/solution.py
@@ -276,20 +276,12 @@
     ahead_low,
     behind_high,
     behind_low,
-    send_taps,
-    send_value,
-    send_grad,
-    got_taps,
-    got_value,
-    got_grad,
+    send,
+    got,
     spec,
     params,
-    out_mix,
-    out_through,
-    out_corr,
-    back_mix,
-    back_through,
-    back_corr,
+    out,
+    back,
     mixed_out,
     grad_gate,
     grad_value,
@@ -301,8 +293,8 @@
 ):
     n = ctx_count * inner_count
     width = value.shape[0]
-    chans = send_value.shape[1]
-    chunks = chans // SUBLANES
+    chunks = send.shape[0]
+    span = n * SUBLANES
     row_count = 2 * inner_count
     half = inner_count + 1
     group_len = width * inner_count
@@ -345,66 +337,65 @@
         return pltpu.make_async_remote_copy(
             src_ref=src,
             dst_ref=dst,
-            send_sem=send_sems.at[kind],
-            recv_sem=recv_sems.at[kind],
+            send_sem=send_sems.at[kind[0], kind[1]],
+            recv_sem=recv_sems.at[kind[0], kind[1]],
             device_id=(lax.div(d, inner_count), lax.rem(d, inner_count)),
             device_id_type=pl.DeviceIdType.MESH,
         )
 
-    def exchange(src, dst, kind, partners, copy):
-        def start(k, carry):
-            copy(k).start()
+    rest = n - inner_count
+    shared = pl.ds(0, 2)
+
+    def start_in(c):
+        def cross(k, carry):
+            group = ctx_idx + 1 + lax.div(k, inner_count)
+            d = lax.rem(group * inner_count + lax.rem(inner_idx + k, inner_count), n)
+            copy_to(send.at[c, d, shared], got.at[c, me, shared], (1, c), d).start()
             return carry
 
-        every = pl.ds(0, partners)
-        whole = copy_to(src.at[every], dst.at[every], kind, lax.rem(me + 1, n))
-        return functools.partial(lax.fori_loop, 1, partners + 1, start, 0), whole
-
-    def everyone(src, dst, kind):
-        def copy(k):
+        def own(k, carry):
+            d = ctx_idx * inner_count + lax.rem(inner_idx + k, inner_count)
+            copy_to(send.at[c, d], got.at[c, me], (0, c), d).start()
+            return carry
+
+        lax.fori_loop(0, rest, cross, 0)
+        lax.fori_loop(1, inner_count, own, 0)
+
+    def start_out(c):
+        def one(k, carry):
             d = lax.rem(me + k, n)
-            return copy_to(src.at[d], dst.at[me], kind, d)
-
-        return exchange(src, dst, kind, n - 1, copy)
-
-    def own_group(src, dst, kind):
-        def copy(k):
-            d = ctx_idx * inner_count + lax.rem(inner_idx + k, inner_count)
-            return copy_to(src.at[d], dst.at[inner_idx], kind, d)
-
-        return exchange(src, dst, kind, inner_count - 1, copy)
-
-    def folded(src, dst, kind):
-        def copy(k):
-            d = lax.rem(me + k, n)
-            return copy_to(src.at[lax.rem(d, inner_count)], dst.at[me], kind, d)
-
-        return exchange(dst, dst, kind, n - 1, copy)
-
-    taps_start, taps_all = own_group(send_taps, got_taps, 0)
-    value_start, value_all = everyone(send_value, got_value, 1)
-    grad_start, grad_all = everyone(send_grad, got_grad, 2)
-    corr_start, corr_all = folded(out_corr, back_corr, 3)
-    mix_start, mix_all = everyone(out_mix, back_mix, 4)
-    through_start, through_all = everyone(out_through, back_through, 5)
+            copy_to(out.at[c, d], back.at[c, me], (2, c), d).start()
+            return carry
+
+        lax.fori_loop(1, n, one, 0)
+
+    other = lax.rem(me + 1, n)
+
+    def all_in(c):
+        few, many = pl.ds(0, inner_count - 1), pl.ds(0, rest)
+        return (
+            copy_to(send.at[c, few], got.at[c, few], (0, c), other),
+            copy_to(send.at[c, many, shared], got.at[c, many, shared], (1, c), other),
+        )
+
+    def all_out(c):
+        every = pl.ds(0, n - 1)
+        return copy_to(out.at[c, every], back.at[c, every], (2, c), other)
 
     def by_channel(block):
-        return jnp.transpose(block).reshape(n, chans, width)
-
-    loads[0].wait()
-    send_taps[...] = by_channel(taps[...])
-    pl.semaphore_wait(barrier, n - 1)
-    taps_start()
-    got_taps[inner_idx] = send_taps[me]
-    loads[1].wait()
-    send_value[...] = by_channel(value[...])
-    value_start()
-    got_value[me] = send_value[me]
-    loads[2].wait()
-    loads[3].wait()
-    send_grad[...] = by_channel(cot[...] * gate[...])
-    grad_start()
-    got_grad[me] = send_grad[me]
+        return jnp.transpose(block).reshape(n, SUBLANES, width)
+
+    for load in loads[:4]:
+        load.wait()
+    for c in range(chunks):
+        cols = slice(c * span, (c + 1) * span)
+        send[c, :, 0] = by_channel(value[:, cols])
+        send[c, :, 1] = by_channel(cot[:, cols] * gate[:, cols])
+        send[c, :, 2] = by_channel(taps[:, cols])
+        if c == 0:
+            pl.semaphore_wait(barrier, n - 1)
+        start_in(c)
+        got[c, me] = send[c, me]
 
     for load in loads[4:]:
         load.wait()
@@ -429,7 +420,7 @@
     lane = lax.broadcasted_iota(jnp.int32, (SUBLANES, width), 1).astype(jnp.float32)
 
     def per_channel(chunk):
-        own = params[pl.ds(pl.multiple_of(me * chans + chunk * SUBLANES, SUBLANES), SUBLANES), :]
+        own = params[pl.ds(pl.multiple_of(chunk * span + me * SUBLANES, SUBLANES), SUBLANES), :]
 
         def wide(column):
             return jnp.broadcast_to(own[:, column : column + 1], (SUBLANES, width))
@@ -441,85 +432,56 @@
         ]
         return rates, coeffs, keeps
 
-    def rows_of(chunk):
-        return pl.ds(pl.multiple_of(chunk * SUBLANES, SUBLANES), SUBLANES)
-
-    def add_tail(chunk, carry):
-        rates, coeffs, _ = per_channel(chunk)
+    def add_tail(c):
+        rates, coeffs, _ = per_channel(c)
         steps = [jnp.exp(-r * float(width)) for r in rates]
-        terms = [c * jnp.exp(-r * lane) for r, c in zip(rates, coeffs)]
-        at = rows_of(chunk)
+        terms = [f * jnp.exp(-r * lane) for r, f in zip(rates, coeffs)]
+        base = ctx_idx * inner_count
         for i in range(inner_count):
-            got_taps[i, at, :] = got_taps[i, at, :] + sum(terms[1:], terms[0])
+            got[c, base + i, 2] = got[c, base + i, 2] + sum(terms[1:], terms[0])
             terms = [t * s for t, s in zip(terms, steps)]
-        return carry
-
-    def rows_ahead(src, base, slot, chunk):
-        at = rows_of(chunk)
+
+    def rows_ahead(c, base, tensor, slot):
         blank = (None, None)
-        xs = [(src[base + i, at, :], None) for i in range(inner_count)] + [blank] * inner_count
+        xs = [(got[c, base + i, tensor], None) for i in range(inner_count)] + [blank] * inner_count
         parts = transform_ahead(xs)
         for k in range(half):
             real, imag = parts[k]
-            c, s = twist[0, k : k + 1, :], twist[1, k : k + 1, :]
+            cosine, sine = twist[0, k : k + 1, :], twist[1, k : k + 1, :]
             if imag is None:
-                first, second = real * c, -(real * s)
+                first, second = real * cosine, -(real * sine)
             else:
-                first, second = real * c + imag * s, imag * c - real * s
-            spec[slot, k, at, :width] = first
-            spec[slot, k, at, width:] = second
-
-    def line(slot, high, low):
-        data = spec[slot].reshape((half + 1) * chans, 2 * width)
+                first, second = real * cosine + imag * sine, imag * cosine - real * sine
+            spec[slot, k, :, :width] = first
+            spec[slot, k, :, width:] = second
+
+    def lines(high, low):
+        data = spec[...].reshape(-1, 2 * width)
         top = data.astype(jnp.bfloat16)
-        rest = (data - top.astype(jnp.float32)).astype(jnp.bfloat16)
+        rest_part = (data - top.astype(jnp.float32)).astype(jnp.bfloat16)
         dot = functools.partial(jnp.dot, preferred_element_type=jnp.float32)
-        result = dot(rest, high[...]) + dot(top, low[...]) + dot(top, high[...])
-        spec[slot] = result.reshape(half + 1, chans, 2 * width)
-
-    def rows_behind(slot, chunk):
-        at = rows_of(chunk)
+        result = dot(rest_part, high[...]) + dot(top, low[...]) + dot(top, high[...])
+        spec[...] = result.reshape(spec.shape)
+
+    def rows_behind(slot):
         xs = []
         for k in range(half):
-            real, imag = spec[slot, k, at, :width], spec[slot, k, at, width:]
-            c, s = twist[2, k : k + 1, :], twist[3, k : k + 1, :]
-            xs.append((real * c - imag * s, real * s + imag * c))
+            real, imag = spec[slot, k, :, :width], spec[slot, k, :, width:]
+            cosine, sine = twist[2, k : k + 1, :], twist[3, k : k + 1, :]
+            xs.append((real * cosine - imag * sine, real * sine + imag * cosine))
         xs += [(None, None)] * (row_count - half)
         return [y[0] for y in transform_behind(xs)[:inner_count]]
 
-    def to_spectra(src, first_slot, groups):
-        def one(step, carry):
-            g = lax.div(step, chunks)
-            rows_ahead(src, g * inner_count, first_slot + g, lax.rem(step, chunks))
-            return carry
-
-        lax.fori_loop(0, groups * chunks, one, 0)
-
-        def transform(g, carry):
-            line(first_slot + g, ahead_high, ahead_low)
-            return carry
-
-        lax.fori_loop(0, groups, transform, 0)
-
-    taps_all.wait_recv()
-    lax.fori_loop(0, chunks, add_tail, 0)
     kern_slot, value_slot, grad_slot = 0, 1, 1 + ctx_count
-    to_spectra(got_taps, kern_slot, 1)
-    value_all.wait_recv()
-    to_spectra(got_value, value_slot, ctx_count)
-    grad_all.wait_recv()
-    to_spectra(got_grad, grad_slot, ctx_count)
-
-    def multiply(step, carry):
-        k = lax.div(step, chunks)
-        at = rows_of(lax.rem(step, chunks))
-
+    grad_scale = 1.0 / math.sqrt(group_len * ctx_count)
+
+    def multiply(k, carry):
         def load(slot):
-            return spec[slot, k, at, :width], spec[slot, k, at, width:]
+            return spec[slot, k, :, :width], spec[slot, k, :, width:]
 
         def store(slot, real, imag):
-            spec[slot, k, at, :width] = real
-            spec[slot, k, at, width:] = imag
+            spec[slot, k, :, :width] = real
+            spec[slot, k, :, width:] = imag
 
         kr, ki = load(kern_slot)
         corr_r = corr_i = 0.0
@@ -533,38 +495,8 @@
         store(kern_slot, corr_r, corr_i)
         return carry
 
-    lax.fori_loop(0, half * chunks, multiply, 0)
-
-    grad_scale = 1.0 / math.sqrt(group_len * ctx_count)
-    line(kern_slot, behind_high, behind_low)
-
-    def corr_rows(chunk, carry):
-        for i, y in enumerate(rows_behind(kern_slot, chunk)):
-            out_corr[i, rows_of(chunk), :] = y * grad_scale
-        return carry
-
-    lax.fori_loop(0, chunks, corr_rows, 0)
-    corr_start()
-    back_corr[me] = out_corr[inner_idx]
-
-    def from_spectra(first_slot, dst):
-        def transform(g, carry):
-            line(first_slot + g, behind_high, behind_low)
-            return carry
-
-        lax.fori_loop(0, ctx_count, transform, 0)
-
-        def one(step, carry):
-            g, chunk = lax.div(step, chunks), lax.rem(step, chunks)
-            for i, y in enumerate(rows_behind(first_slot + g, chunk)):
-                dst[g * inner_count + i, rows_of(chunk), :] = y
-            return carry
-
-        lax.fori_loop(0, ctx_count * chunks, one, 0)
-
-    def carried_ahead(chunk, carry):
+    def carried_ahead(chunk):
         rates, coeffs, keeps = per_channel(chunk)
-        at = rows_of(chunk)
         steps = [jnp.exp(-r * float(width)) for r in rates]
         whole = [jnp.exp(-r * float(group_len)) for r in rates]
         to_end = [jnp.exp(-r * (width - 1.0 - lane)) for r in rates]
@@ -573,7 +505,7 @@
         for g in range(ctx_count - 1):
             acc = [jnp.zeros((SUBLANES, width), jnp.float32)] * modes
             for i in range(inner_count):
-                block = got_value[g * inner_count + i, at, :]
+                block = got[chunk, g * inner_count + i, 0]
                 acc = [a * s + block for a, s in zip(acc, steps)]
             for m in range(modes):
                 total = jnp.sum(acc[m] * to_end[m], 1, keepdims=True)
@@ -581,13 +513,11 @@
             terms = [f * st for f, st in zip(from_start, state)]
             for i in range(inner_count):
                 row = (g + 1) * inner_count + i
-                out_mix[row, at, :] = out_mix[row, at, :] + sum(terms[1:], terms[0])
+                out[chunk, row, 0] = out[chunk, row, 0] + sum(terms[1:], terms[0])
                 terms = [t * s for t, s in zip(terms, steps)]
-        return carry
-
-    def carried_behind(chunk, carry):
+
+    def carried_behind(chunk):
         rates, coeffs, keeps = per_channel(chunk)
-        at = rows_of(chunk)
         steps = [jnp.exp(-r * float(width)) for r in rates]
         whole = [jnp.exp(-r * float(group_len)) for r in rates]
         to_end = [jnp.exp(-r * (width - 1.0 - lane)) for r in rates]
@@ -596,7 +526,7 @@
         for g in reversed(range(1, ctx_count)):
             acc = [jnp.zeros((SUBLANES, width), jnp.float32)] * modes
             for i in reversed(range(inner_count)):
-                block = got_grad[g * inner_count + i, at, :]
+                block = got[chunk, g * inner_count + i, 1]
                 acc = [a * s + block for a, s in zip(acc, steps)]
             for m in range(modes):
                 total = jnp.sum(acc[m] * from_start[m], 1, keepdims=True)
@@ -609,65 +539,91 @@
             ]
             for i in reversed(range(inner_count)):
                 row = (g - 1) * inner_count + i
-                out_through[row, at, :] = out_through[row, at, :] + sum(terms[1:], terms[0])
+                out[chunk, row, 1] = out[chunk, row, 1] + sum(terms[1:], terms[0])
                 terms = [t * s for t, s in zip(terms, steps)]
+
+    def process(c, carry):
+        for whole in all_in(c):
+            whole.wait_recv()
+        add_tail(c)
+        rows_ahead(c, ctx_idx * inner_count, 2, kern_slot)
+
+        def ahead(step, inner_carry):
+            tensor, g = lax.div(step, ctx_count), lax.rem(step, ctx_count)
+            rows_ahead(c, g * inner_count, tensor, 1 + step)
+            return inner_carry
+
+        lax.fori_loop(0, 2 * ctx_count, ahead, 0)
+        lines(ahead_high, ahead_low)
+        lax.fori_loop(0, half, multiply, 0)
+        lines(behind_high, behind_low)
+        for i, y in enumerate(rows_behind(kern_slot)):
+            y = y * grad_scale
+            for g in range(ctx_count):
+                out[c, g * inner_count + i, 2] = y
+
+        def behind(step, inner_carry):
+            tensor, g = lax.div(step, ctx_count), lax.rem(step, ctx_count)
+            for i, y in enumerate(rows_behind(1 + step)):
+                out[c, g * inner_count + i, tensor] = y
+            return inner_carry
+
+        lax.fori_loop(0, 2 * ctx_count, behind, 0)
+        carried_ahead(c)
+        carried_behind(c)
+        start_out(c)
+        back[c, me] = out[c, me]
         return carry
 
-    from_spectra(value_slot, out_mix)
-    lax.fori_loop(0, chunks, carried_ahead, 0)
-    mix_start()
-    back_mix[me] = out_mix[me]
-    from_spectra(grad_slot, out_through)
-    lax.fori_loop(0, chunks, carried_behind, 0)
-    through_start()
-    back_through[me] = out_through[me]
-
-    def by_token(blocks):
-        return jnp.transpose(blocks[...].reshape(n * chans, width))
-
-    corr_all.wait_recv()
-    stores = [
-        pltpu.make_async_copy(src, dst, store_sems.at[i])
-        for i, (src, dst) in enumerate(
-            (
-                (mixed_out, mixed_hbm),
-                (grad_gate, gated_hbm),
-                (grad_value, turned_hbm),
-                (grad_filter, filtered_hbm),
-            )
-        )
-    ]
-    grad_filter[...] = by_token(back_corr)
-    stores[3].start()
-    mix_all.wait_recv()
-    mixture = by_token(back_mix)
-    mixed_out[...] = gate[...] * mixture
-    stores[0].start()
-    grad_gate[...] = cot[...] * mixture
-    stores[1].start()
-    through_all.wait_recv()
-    grad_value[...] = by_token(back_through)
-    stores[2].start()
-    for whole in (taps_all, value_all, grad_all, corr_all, mix_all, through_all):
-        whole.wait_send()
+    lax.fori_loop(0, chunks, process, 0)
+
+    def by_token(c, tensor):
+        return jnp.transpose(back[c, :, tensor].reshape(span, width))
+
+    stores = []
+    for c in range(chunks):
+        cols = slice(c * span, (c + 1) * span)
+        all_out(c).wait_recv()
+        mixture = by_token(c, 0)
+        mixed_out[:, cols] = gate[:, cols] * mixture
+        grad_gate[:, cols] = cot[:, cols] * mixture
+        grad_value[:, cols] = by_token(c, 1)
+        grad_filter[:, cols] = by_token(c, 2)
+        moves = (
+            (mixed_out, mixed_hbm),
+            (grad_gate, gated_hbm),
+            (grad_value, turned_hbm),
+            (grad_filter, filtered_hbm),
+        )
+        for i, (src, dst) in enumerate(moves):
+            part = pl.ds(c * span, span)
+            store = pltpu.make_async_copy(src.at[:, part], dst.at[:, part], store_sems.at[i, c])
+            store.start()
+            stores.append(store)
+    for c in range(chunks):
+        for whole in all_in(c) + (all_out(c),):
+            whole.wait_send()
     for store in stores:
         store.wait()
 
 
-def finish_kernel(pieces, *refs):
-    sources, targets, sems = refs[:4], refs[4:8], refs[8]
-    rows = sources[0].shape[0] // pieces
-    copies = [
-        pltpu.make_async_copy(
-            src.at[pl.ds(p * rows, rows)], dst.at[pl.ds(p * rows, rows)], sems.at[i, p]
-        )
-        for i, (src, dst) in enumerate(zip(sources, targets))
-        for p in range(pieces)
+def finish_kernel(*refs):
+    sources, targets, held, load_sems, store_sems = refs[:4], refs[4:8], refs[8:12], refs[12], refs[13]
+    loads = [
+        pltpu.make_async_copy(src, mid, load_sems.at[i])
+        for i, (src, mid) in enumerate(zip(sources, held))
     ]
-    for copy in copies:
-        copy.start()
-    for copy in copies:
-        copy.wait()
+    stores = [
+        pltpu.make_async_copy(mid, dst, store_sems.at[i])
+        for i, (mid, dst) in enumerate(zip(held, targets))
+    ]
+    for load in loads:
+        load.start()
+    for load, store in zip(loads, stores):
+        load.wait()
+        store.start()
+    for store in stores:
+        store.wait()
 
 
 def fits(mesh, value_input):
@@ -675,6 +631,7 @@
     tok_dev, channels = value_input.shape
     return (
         tok_dev == LANES
+        and ctx_count > 1
         and channels % (inner_count * ctx_count * SUBLANES) == 0
         and inner_count & (inner_count - 1) == 0
     )
@@ -687,13 +644,13 @@
     n = inner_count * ctx_count
     tok_dev, channels = value_input.shape
     modes = decay_rate.shape[0]
-    chans = channels // n
+    chunks = channels // (n * SUBLANES)
     half = inner_count + 1
     tables = line_tables(tok_dev, 2 * inner_count, half)
     keep_rows = boundary_keep.reshape(-1, channels)
     block = jax.ShapeDtypeStruct((tok_dev, channels), jnp.float32)
     f32 = functools.partial(pltpu.VMEM, dtype=jnp.float32)
-    pieces, own_pieces = f32((n, chans, tok_dev)), f32((inner_count, chans, tok_dev))
+    pieces = f32((chunks, n, 3, SUBLANES, tok_dev))
     hbm = pl.BlockSpec(memory_space=pltpu.HBM)
     operands = (
         gate_input,
@@ -715,36 +672,29 @@
         + [
             pieces,
             pieces,
-            pieces,
-            own_pieces,
-            pieces,
-            pieces,
-            f32((1 + 2 * ctx_count, half + 1, chans, 2 * tok_dev)),
+            f32((1 + 2 * ctx_count, half + 1, SUBLANES, 2 * tok_dev)),
             f32((channels, LANES)),
-            pieces,
-            pieces,
-            own_pieces,
-            pieces,
             pieces,
             pieces,
         ]
         + [f32((tok_dev, channels))] * 4
         + [
             pltpu.SemaphoreType.DMA((len(operands),)),
-            pltpu.SemaphoreType.DMA((4,)),
-            pltpu.SemaphoreType.DMA((6,)),
-            pltpu.SemaphoreType.DMA((6,)),
+            pltpu.SemaphoreType.DMA((4, chunks)),
+            pltpu.SemaphoreType.DMA((3, chunks)),
+            pltpu.SemaphoreType.DMA((3, chunks)),
         ],
         compiler_params=pltpu.CompilerParams(
             collective_id=0, has_side_effects=True, vmem_limit_bytes=60 * 1024 * 1024
         ),
     )(*operands)
     return pl.pallas_call(
-        functools.partial(finish_kernel, 2),
+        finish_kernel,
         out_shape=(block,) * 4,
         in_specs=[hbm] * 4,
         out_specs=(hbm,) * 4,
-        scratch_shapes=[pltpu.SemaphoreType.DMA((4, 2))],
+        scratch_shapes=[f32((tok_dev, channels))] * 4
+        + [pltpu.SemaphoreType.DMA((4,)), pltpu.SemaphoreType.DMA((4,))],
         compiler_params=pltpu.CompilerParams(vmem_limit_bytes=60 * 1024 * 1024),
     )(*results)
 

time: 110 us -> 58 us (0.53)
  Pallas kernels: 109 us -> 57.2 us
    pallas_call x1, Pallas kernels: 48.8 us -> 2.2 us  [shards_by_channel(): pl.pallas_call(finish_kernel, out_shape=(block,) * 4, in_specs=[hbm] * 4,...]
    pallas_call x1, Pallas kernels: 60.3 us -> 55 us  [shards_by_channel(): pl.pallas_call(functools.partial(mixer_kernel, ctx_count, inner_count, mo...]
where the time goes in v3:
time: 58 us; the launch traced here: 57.8 us
  Pallas kernels  57.2 us (99%)
  between operations  0.64 us (1%)
    pallas_call x1, Pallas kernels, shards_by_channel(): pl.pallas_call(functools.partial(mixer_kernel, ctx_count, inner_count, mo...  55 us
    pallas_call x1, Pallas kernels, shards_by_channel(): pl.pallas_call(finish_kernel, out_shape=(block,) * 4, in_specs=[hbm] * 4,...  2.2 us

profile of v3, /device:TPU:0, one launch (start us, length us, event | category | flops | bytes accessed | tf_op | source)
XLA Modules:
  0.0 57.8 jit_solution(5883698681747473620)
XLA Ops:
  0.6 55.0 %shard_map.120 = (f32[128,768]{1,0:T(8,128)}, f32[128,768]{1,0:T(8,128)}, f32[128,768]{1,0:T(8,128)}, f32[128,768]{1,0:T(8,128)}) custom-call(f32[128,768]{1,0:T(8,128)} %gate_hbm.1, f32[128,768]{1,0:T(8,128)} %value_hbm.1, f32[128,768]{1,0:T(8,128)} %taps_hbm.1, f32[8,768]{1,0:T(8,128)} %rate_hbm.1, f32[8,768]{1,0:T(8,128)} %coeff_hbm.1, f32[8,768]{1,0:T(8,128)} %bitcast.1, ...), custom_call_target="tpu_custom_call" | custom-call | tf_op jit(solution)/shard_map/pallas_call | solution.py:665
  55.6 2.2 %shard_map.121 = (f32[128,768]{1,0:T(8,128)}, f32[128,768]{1,0:T(8,128)}, f32[128,768]{1,0:T(8,128)}, f32[128,768]{1,0:T(8,128)}) custom-call(f32[128,768]{1,0:T(8,128)} %get-tuple-element.8.refs_0_, f32[128,768]{1,0:T(8,128)} %get-tuple-element.9.refs_1_, f32[128,768]{1,0:T(8,128)} %get-tuple-element.10.refs_2_, f32[128,768]{1,0:T(8,128)} %get-tuple-element.11.refs_3_), custom_call_target="tpu_custom_call" | custom-call | tf_op jit(solution)/shard_map/pallas_call | solution.py:691

commit v4 on v3

--- a/solution.py
+++ b/solution.py
@@ -344,43 +344,54 @@
         )
 
     rest = n - inner_count
-    shared = pl.ds(0, 2)
-
-    def start_in(c):
+    other = lax.rem(me + 1, n)
+
+    def spread(src, dst, c, kind, tensors):
         def cross(k, carry):
             group = ctx_idx + 1 + lax.div(k, inner_count)
             d = lax.rem(group * inner_count + lax.rem(inner_idx + k, inner_count), n)
-            copy_to(send.at[c, d, shared], got.at[c, me, shared], (1, c), d).start()
+            copy_to(src.at[c, d, tensors], dst.at[c, me, tensors], (kind + 1, c), d).start()
             return carry
 
         def own(k, carry):
             d = ctx_idx * inner_count + lax.rem(inner_idx + k, inner_count)
-            copy_to(send.at[c, d], got.at[c, me], (0, c), d).start()
+            copy_to(src.at[c, d], dst.at[c, me], (kind, c), d).start()
             return carry
 
         lax.fori_loop(0, rest, cross, 0)
         lax.fori_loop(1, inner_count, own, 0)
 
-    def start_out(c):
-        def one(k, carry):
-            d = lax.rem(me + k, n)
-            copy_to(out.at[c, d], back.at[c, me], (2, c), d).start()
-            return carry
-
-        lax.fori_loop(1, n, one, 0)
-
-    other = lax.rem(me + 1, n)
-
-    def all_in(c):
+    def spread_all(src, dst, c, kind, tensors):
         few, many = pl.ds(0, inner_count - 1), pl.ds(0, rest)
         return (
-            copy_to(send.at[c, few], got.at[c, few], (0, c), other),
-            copy_to(send.at[c, many, shared], got.at[c, many, shared], (1, c), other),
-        )
+            copy_to(src.at[c, few], dst.at[c, few], (kind, c), other),
+            copy_to(src.at[c, many, tensors], dst.at[c, many, tensors], (kind + 1, c), other),
+        )
+
+    shared, full = pl.ds(0, 2), pl.ds(0, 3)
+
+    def start_in(c):
+        spread(send, got, c, 0, shared)
+
+    def all_in(c):
+        return spread_all(send, got, c, 0, shared)
 
     def all_out(c):
-        every = pl.ds(0, n - 1)
-        return copy_to(out.at[c, every], back.at[c, every], (2, c), other)
+        return spread_all(out, back, c, 2, full if c == chunks - 1 else shared)
+
+    def relays(c):
+        if c == chunks - 1:
+            return []
+        group = pl.ds(pl.multiple_of(ctx_idx * inner_count, inner_count), inner_count)
+        return [
+            copy_to(
+                back.at[c, group, 2],
+                back.at[c, group, 2],
+                (3 + p, c),
+                lax.rem(me + p * inner_count, n),
+            )
+            for p in range(1, ctx_count)
+        ]
 
     def by_channel(block):
         return jnp.transpose(block).reshape(n, SUBLANES, width)
@@ -571,8 +582,16 @@
         lax.fori_loop(0, 2 * ctx_count, behind, 0)
         carried_ahead(c)
         carried_behind(c)
-        start_out(c)
         back[c, me] = out[c, me]
+
+        @pl.when(c < chunks - 1)
+        def _():
+            spread(out, back, c, 2, shared)
+
+        @pl.when(c == chunks - 1)
+        def _():
+            spread(out, back, c, 2, full)
+
         return carry
 
     lax.fori_loop(0, chunks, process, 0)
@@ -580,14 +599,23 @@
     def by_token(c, tensor):
         return jnp.transpose(back[c, :, tensor].reshape(span, width))
 
+    for c in range(chunks):
+        if c < chunks - 1:
+            all_out(c)[0].wait_recv()
+        for relay in relays(c):
+            relay.start()
     stores = []
     for c in range(chunks):
         cols = slice(c * span, (c + 1) * span)
-        all_out(c).wait_recv()
+        if c == chunks - 1:
+            all_out(c)[0].wait_recv()
+        all_out(c)[1].wait_recv()
         mixture = by_token(c, 0)
         mixed_out[:, cols] = gate[:, cols] * mixture
         grad_gate[:, cols] = cot[:, cols] * mixture
         grad_value[:, cols] = by_token(c, 1)
+        for relay in relays(c):
+            relay.wait_recv()
         grad_filter[:, cols] = by_token(c, 2)
         moves = (
             (mixed_out, mixed_hbm),
@@ -601,7 +629,7 @@
             store.start()
             stores.append(store)
     for c in range(chunks):
-        for whole in all_in(c) + (all_out(c),):
+        for whole in (*all_in(c), *all_out(c), *relays(c)):
             whole.wait_send()
     for store in stores:
         store.wait()
@@ -681,8 +709,8 @@
         + [
             pltpu.SemaphoreType.DMA((len(operands),)),
             pltpu.SemaphoreType.DMA((4, chunks)),
-            pltpu.SemaphoreType.DMA((3, chunks)),
-            pltpu.SemaphoreType.DMA((3, chunks)),
+            pltpu.SemaphoreType.DMA((3 + ctx_count, chunks)),
+            pltpu.SemaphoreType.DMA((3 + ctx_count, chunks)),
         ],
         compiler_params=pltpu.CompilerParams(
             collective_id=0, has_side_effects=True, vmem_limit_bytes=60 * 1024 * 1024

time: 58 us -> 55.3 us (0.953)
  Pallas kernels: 57.2 us -> 54.5 us
    pallas_call x1, Pallas kernels: 55 us -> 52.3 us  [shards_by_channel(): pl.pallas_call(functools.partial(mixer_kernel, ctx_count, inner_count, mo...]
where the time goes in v4:
time: 55.3 us; the launch traced here: 55.1 us
  Pallas kernels  54.5 us (99%)
  between operations  0.64 us (1%)
    pallas_call x1, Pallas kernels, shards_by_channel(): pl.pallas_call(functools.partial(mixer_kernel, ctx_count, inner_count, mo...  52.3 us
    pallas_call x1, Pallas kernels, shards_by_channel(): pl.pallas_call(finish_kernel, out_shape=(block,) * 4, in_specs=[hbm] * 4,...  2.2 us

profile of v4, /device:TPU:0, one launch (start us, length us, event | category | flops | bytes accessed | tf_op | source)
XLA Modules:
  0.0 55.1 jit_solution(5285520526802144885)
XLA Ops:
  0.6 52.3 %shard_map.120 = (f32[128,768]{1,0:T(8,128)}, f32[128,768]{1,0:T(8,128)}, f32[128,768]{1,0:T(8,128)}, f32[128,768]{1,0:T(8,128)}) custom-call(f32[128,768]{1,0:T(8,128)} %gate_hbm.1, f32[128,768]{1,0:T(8,128)} %value_hbm.1, f32[128,768]{1,0:T(8,128)} %taps_hbm.1, f32[8,768]{1,0:T(8,128)} %rate_hbm.1, f32[8,768]{1,0:T(8,128)} %coeff_hbm.1, f32[8,768]{1,0:T(8,128)} %bitcast.1, ...), custom_call_target="tpu_custom_call" | custom-call | tf_op jit(solution)/shard_map/pallas_call | solution.py:693
  52.9 2.2 %shard_map.121 = (f32[128,768]{1,0:T(8,128)}, f32[128,768]{1,0:T(8,128)}, f32[128,768]{1,0:T(8,128)}, f32[128,768]{1,0:T(8,128)}) custom-call(f32[128,768]{1,0:T(8,128)} %get-tuple-element.8.refs_0_, f32[128,768]{1,0:T(8,128)} %get-tuple-element.9.refs_1_, f32[128,768]{1,0:T(8,128)} %get-tuple-element.10.refs_2_, f32[128,768]{1,0:T(8,128)} %get-tuple-element.11.refs_3_), custom_call_target="tpu_custom_call" | custom-call | tf_op jit(solution)/shard_map/pallas_call | solution.py:719

commit v5 on v4

--- a/solution.py
+++ b/solution.py
@@ -349,12 +349,14 @@
     def spread(src, dst, c, kind, tensors):
         def cross(k, carry):
             group = ctx_idx + 1 + lax.div(k, inner_count)
-            d = lax.rem(group * inner_count + lax.rem(inner_idx + k, inner_count), n)
+            place = lax.rem(inner_idx + inner_count // 2 + k, inner_count)
+            d = lax.rem(group * inner_count + place, n)
             copy_to(src.at[c, d, tensors], dst.at[c, me, tensors], (kind + 1, c), d).start()
             return carry
 
         def own(k, carry):
-            d = ctx_idx * inner_count + lax.rem(inner_idx + k, inner_count)
+            shift = 1 + lax.rem(k + inner_count // 2 - 2, inner_count - 1)
+            d = ctx_idx * inner_count + lax.rem(inner_idx + shift, inner_count)
             copy_to(src.at[c, d], dst.at[c, me], (kind, c), d).start()
             return carry
 

time: 55.3 us -> 56.5 us (1.022)
  Pallas kernels: 54.5 us -> 55.7 us
    pallas_call x1, Pallas kernels: 52.3 us -> 53.5 us  [shards_by_channel(): pl.pallas_call(functools.partial(mixer_kernel, ctx_count, inner_count, mo...]
where the time goes in v5:
time: 56.5 us; the launch traced here: 56.4 us
  Pallas kernels  55.7 us (99%)
  between operations  0.64 us (1%)
    pallas_call x1, Pallas kernels, shards_by_channel(): pl.pallas_call(functools.partial(mixer_kernel, ctx_count, inner_count, mo...  53.5 us
    pallas_call x1, Pallas kernels, shards_by_channel(): pl.pallas_call(finish_kernel, out_shape=(block,) * 4, in_specs=[hbm] * 4,...  2.2 us

profile of v5, /device:TPU:0, one launch (start us, length us, event | category | flops | bytes accessed | tf_op | source)
XLA Modules:
  0.0 56.4 jit_solution(2699380017037638792)
XLA Ops:
  0.6 53.5 %shard_map.120 = (f32[128,768]{1,0:T(8,128)}, f32[128,768]{1,0:T(8,128)}, f32[128,768]{1,0:T(8,128)}, f32[128,768]{1,0:T(8,128)}) custom-call(f32[128,768]{1,0:T(8,128)} %gate_hbm.1, f32[128,768]{1,0:T(8,128)} %value_hbm.1, f32[128,768]{1,0:T(8,128)} %taps_hbm.1, f32[8,768]{1,0:T(8,128)} %rate_hbm.1, f32[8,768]{1,0:T(8,128)} %coeff_hbm.1, f32[8,768]{1,0:T(8,128)} %bitcast.1, ...), custom_call_target="tpu_custom_call" | custom-call | tf_op jit(solution)/shard_map/pallas_call | solution.py:695
  54.2 2.2 %shard_map.121 = (f32[128,768]{1,0:T(8,128)}, f32[128,768]{1,0:T(8,128)}, f32[128,768]{1,0:T(8,128)}, f32[128,768]{1,0:T(8,128)}) custom-call(f32[128,768]{1,0:T(8,128)} %get-tuple-element.8.refs_0_, f32[128,768]{1,0:T(8,128)} %get-tuple-element.9.refs_1_, f32[128,768]{1,0:T(8,128)} %get-tuple-element.10.refs_2_, f32[128,768]{1,0:T(8,128)} %get-tuple-element.11.refs_3_), custom_call_target="tpu_custom_call" | custom-call | tf_op jit(solution)/shard_map/pallas_call | solution.py:721

commit v6 on v4

--- a/solution.py
+++ b/solution.py
@@ -286,6 +286,7 @@
     grad_gate,
     grad_value,
     grad_filter,
+    block_sems,
     load_sems,
     store_sems,
     send_sems,
@@ -302,11 +303,17 @@
     inner_idx = lax.axis_index("inner")
     me = ctx_idx * inner_count + inner_idx
 
+    blocks = ((taps_hbm, taps), (value_hbm, value), (gate_hbm, gate), (cot_hbm, cot))
+    block_loads = [
+        [
+            pltpu.make_async_copy(
+                src.at[:, pl.ds(c * span, span)], dst.at[:, pl.ds(c * span, span)], block_sems.at[i, c]
+            )
+            for i, (src, dst) in enumerate(blocks)
+        ]
+        for c in range(chunks)
+    ]
     pairs = (
-        (taps_hbm, taps),
-        (value_hbm, value),
-        (gate_hbm, gate),
-        (cot_hbm, cot),
         (rate_hbm, rate),
         (coeff_hbm, coeff),
         (keep_hbm, keep),
@@ -316,7 +323,7 @@
     loads = [
         pltpu.make_async_copy(src, dst, load_sems.at[i]) for i, (src, dst) in enumerate(pairs)
     ]
-    for load in loads:
+    for load in sum(block_loads, []) + loads:
         load.start()
 
     barrier = pltpu.get_barrier_semaphore()
@@ -396,10 +403,10 @@
     def by_channel(block):
         return jnp.transpose(block).reshape(n, SUBLANES, width)
 
-    for load in loads[:4]:
-        load.wait()
     for c in range(chunks):
         cols = slice(c * span, (c + 1) * span)
+        for load in block_loads[c]:
+            load.wait()
         send[c, :, 0] = by_channel(value[:, cols])
         send[c, :, 1] = by_channel(cot[:, cols] * gate[:, cols])
         send[c, :, 2] = by_channel(taps[:, cols])
@@ -408,7 +415,7 @@
         start_in(c)
         got[c, me] = send[c, me]
 
-    for load in loads[4:]:
+    for load in loads:
         load.wait()
     rows = [rate[...], coeff[...], keep[...]]
     filled = sum(r.shape[0] for r in rows)
@@ -707,6 +714,7 @@
         ]
         + [f32((tok_dev, channels))] * 4
         + [
+            pltpu.SemaphoreType.DMA((4, chunks)),
             pltpu.SemaphoreType.DMA((len(operands),)),
             pltpu.SemaphoreType.DMA((4, chunks)),
             pltpu.SemaphoreType.DMA((3 + ctx_count, chunks)),

time: 55.3 us -> 55.1 us (level)
  no operation moved by 1% of the time
where the time goes in v6:
time: 55.1 us; the launch traced here: 54.9 us
  Pallas kernels  54.3 us (99%)
  between operations  0.64 us (1%)
    pallas_call x1, Pallas kernels, shards_by_channel(): pl.pallas_call(functools.partial(mixer_kernel, ctx_count, inner_count, mo...  52.1 us
    pallas_call x1, Pallas kernels, shards_by_channel(): pl.pallas_call(finish_kernel, out_shape=(block,) * 4, in_specs=[hbm] * 4,...  2.2 us

profile of v6, /device:TPU:0, one launch (start us, length us, event | category | flops | bytes accessed | tf_op | source)
XLA Modules:
  0.0 54.9 jit_solution(11970446978984883187)
XLA Ops:
  0.6 52.1 %shard_map.120 = (f32[128,768]{1,0:T(8,128)}, f32[128,768]{1,0:T(8,128)}, f32[128,768]{1,0:T(8,128)}, f32[128,768]{1,0:T(8,128)}) custom-call(f32[128,768]{1,0:T(8,128)} %gate_hbm.1, f32[128,768]{1,0:T(8,128)} %value_hbm.1, f32[128,768]{1,0:T(8,128)} %taps_hbm.1, f32[8,768]{1,0:T(8,128)} %rate_hbm.1, f32[8,768]{1,0:T(8,128)} %coeff_hbm.1, f32[8,768]{1,0:T(8,128)} %bitcast.1, ...), custom_call_target="tpu_custom_call" | custom-call | tf_op jit(solution)/shard_map/pallas_call | solution.py:700
  52.7 2.2 %shard_map.121 = (f32[128,768]{1,0:T(8,128)}, f32[128,768]{1,0:T(8,128)}, f32[128,768]{1,0:T(8,128)}, f32[128,768]{1,0:T(8,128)}) custom-call(f32[128,768]{1,0:T(8,128)} %get-tuple-element.8.refs_0_, f32[128,768]{1,0:T(8,128)} %get-tuple-element.9.refs_1_, f32[128,768]{1,0:T(8,128)} %get-tuple-element.10.refs_2_, f32[128,768]{1,0:T(8,128)} %get-tuple-element.11.refs_3_), custom_call_target="tpu_custom_call" | custom-call | tf_op jit(solution)/shard_map/pallas_call | solution.py:727
